TPU v7x, 128 devices: a whole 4x4x4 slice. The times are simulated.
128 devices in a mesh: row: 8 (over y, core), col: 16 (over z, x).
Axes of the slice: x: 4, y: 4, z: 4, core: 2. Of those that a mesh axis runs over, the one named last changes fastest.
Arguments:
- child_fronts: float32 [20, 512, 20, 1024], P(None, 'col', None, 'row'), as said below
- parent_diagonal: float32 [16384], replicated, may hold values from 0.5 to 4
- block_maps: int32 [2, 20], replicated, may hold values from 0 to 31, as said below
Outputs:
- factored: float32 [16384, 16384], P('row', 'col')
Inputs may be any that keep to these rules, and one draw needn't show every extreme that they name: `child_fronts`: each child's matrix is symmetric and positive definite. `block_maps`: each row names 20 distinct front blocks in increasing order; every one of the 32 front blocks is named by at least one row, and exactly 8 of them by both rows.
All inputs are finite; a program needn't handle non-finite values.
Results may differ from a plain program's by a relative error of at most 0.0001.
Values sent between devices are 32-bit elements; how exact they have to be, the bound alone decides.
No kernel may reach another device: no remote copies, remote signals or barrier semaphores. Data moves between devices by JAX's collectives and lax.ppermute only.
A program may use at most 128 MiB of HBM per device.

v0:
```python
import jax
import jax.numpy as jnp
from jax import lax
from jax.sharding import PartitionSpec as P

B = 512


def broadcast(x, axis, root):
    mine = lax.axis_index(axis) == root
    return lax.psum(jnp.where(mine, x, jnp.zeros_like(x)), axis)


def inverse_maps(block_maps, count):
    blocks = jnp.arange(count, dtype=jnp.int32)
    matches = block_maps[:, None, :] == blocks[None, :, None]
    present = jnp.any(matches, axis=2)
    places = jnp.arange(block_maps.shape[1], dtype=jnp.int32)
    source = jnp.sum(jnp.where(matches, places[None, None, :], 0), axis=2)
    return (source, present)


def shards(child_fronts, parent_diagonal, block_maps):
    row_count = lax.axis_size("row")
    column_count = lax.axis_size("col")
    row_index = lax.axis_index("row")
    column_index = lax.axis_index("col")
    half_count = row_count // 2
    blocks = parent_diagonal.shape[0] // B
    local_rows = blocks // row_count
    local_cols = blocks // column_count
    slice_rows = B // column_count
    slice_cols = 2 * B // row_count
    source, present = inverse_maps(block_maps, blocks)
    my_child = row_index // half_count
    my_source = lax.dynamic_index_in_dim(source, my_child, 0, keepdims=False)
    my_present = lax.dynamic_index_in_dim(present, my_child, 0, keepdims=False)
    picked_rows = jnp.take(child_fronts, my_source, axis=0)
    picked_both = jnp.take(picked_rows, my_source, axis=2)
    keep_mask = my_present[:, None, None, None] & my_present[None, None, :, None]
    picked_both = jnp.where(keep_mask, picked_both, 0.0)
    buffer = picked_both.reshape(
        local_rows, row_count, slice_rows, local_cols, column_count, slice_cols
    )
    buffer = buffer.transpose(1, 4, 0, 2, 3, 5).reshape(row_count * column_count, -1)
    received = lax.all_to_all(buffer, ("row", "col"), split_axis=0, concat_axis=0, tiled=True)
    received = received.reshape(
        2, half_count, column_count, local_rows, slice_rows, local_cols, slice_cols
    )
    summed = received[0] + received[1]
    frontal = summed.transpose(2, 1, 3, 4, 0, 5).reshape(local_rows, B, local_cols, B)
    row_blocks = jnp.arange(local_rows, dtype=jnp.int32) * row_count + row_index
    col_blocks = jnp.arange(local_cols, dtype=jnp.int32) * column_count + column_index
    diag_table = parent_diagonal.reshape(blocks, B)
    diag_rows = jnp.take(diag_table, row_blocks, axis=0)
    same_block = row_blocks[:, None] == col_blocks[None, :]
    identity = jnp.arange(B)[:, None] == jnp.arange(B)[None, :]
    diag_mask = same_block[:, None, :, None] & identity[None, :, None, :]
    frontal = frontal + jnp.where(diag_mask, diag_rows[:, :, None, None], 0.0)
    for panel_index in range(2):
        column_slab = frontal[:, :, panel_index // column_count, :]
        root_row = panel_index % row_count
        local_row = panel_index // row_count
        root_col = panel_index % column_count
        diagonal = broadcast(column_slab[local_row], "row", root_row)
        lower_factor = jnp.linalg.cholesky(diagonal)
        solved = jax.scipy.linalg.solve_triangular(
            lower_factor, column_slab.reshape(-1, B).T, lower=True
        ).T
        solved = solved.reshape(local_rows, B, B)
        factor_factor_column = jnp.where(
            (row_blocks > panel_index)[:, None, None],
            solved,
            jnp.where((row_blocks == panel_index)[:, None, None], lower_factor[None], 0.0),
        )
        factor_factor_column = broadcast(factor_factor_column, "col", root_col)
        owner_rows = (
            jnp.arange(local_cols, dtype=jnp.int32) * column_count + column_index
        ) // row_count
        factor_picked_rows = jnp.take(factor_factor_column, owner_rows, axis=0)
        factor_across = broadcast(factor_picked_rows, "row", column_index % row_count)
        section = frontal
        span_count = local_cols - 0
        product = lax.dot_general(
            factor_factor_column.reshape(-1, B),
            factor_across.reshape(-1, B),
            (((1,), (1,)), ((), ())),
            precision=lax.Precision.HIGHEST,
            preferred_element_type=jnp.float32,
        )
        product = product.reshape(local_rows, B, span_count, B)
        inside = (row_blocks > panel_index)[:, None, None, None] & (col_blocks > panel_index)[
            None, None, :, None
        ]
        section = jnp.where(inside, section - product, section)
        section = jnp.where(
            (col_blocks == panel_index)[None, None, :, None],
            factor_factor_column[:, :, None, :],
            section,
        )
        upper_mask = (row_blocks == panel_index)[:, None, None, None] & (col_blocks > panel_index)[
            None, None, :, None
        ]
        section = jnp.where(upper_mask, 0.0, section)
        frontal = frontal.at[:, :, 0:local_cols, :].set(section)
    return frontal.reshape(local_rows * B, local_cols * B)


def solution(mesh):
    return jax.shard_map(
        shards,
        mesh=mesh,
        in_specs=(P(None, "col", None, "row"), P(), P()),
        out_specs=P("row", "col"),
        check_vma=False,
    )
```

profile of v0, /device:TPU:12, one launch (start us, length us, event | category | flops | bytes accessed | tf_op | source)
XLA Modules:
  0.0 1232.3 jit_solution(6929566411655299351)
XLA Ops:
  7.6 8.1 gather_fusion
  15.6 10.1 broadcast_select_fusion
  25.7 12.2 gather_fusion.1
  38.7 29.2 %fusion = f32[4,8,32,2,16,128]{5,3,2,0,4,1:T(2,128)} fusion(f32[4,8,32,2,16,128]{5,2,1,0,4,3:T(8,128)} %bitcast.155, pred[2,16]{0,1:T(8,128)(4,1)S(1)} %copy.53, pred[4,8,2,16]{2,0,3,1:T(4,128)(4,1)S(1)} %broadcast_and_fusion), kind=kLoop, calls=%fused_computation.10 | loop fusion | flops 8388608 | bytes 33555488 | tf_op jit(solution)/shard_map/jit(_where)/select_n | solution.py:41
  67.9 10.8 all-to-all-start
  80.0 245.6 %all-to-all-done = f32[128,1,32768]{2,1,0:T(1,128)} async-done(((f32[128,1,32768]{2,1,0:T(1,128)}), f32[128,1,32768]{2,1,0:T(1,128)}, u32[]{:S(2)}, u32[]{:S(2)}) %all-to-all-start) | async-done | bytes 16777248 | tf_op jit(solution)/shard_map/all_to_all | solution.py:46
  325.6 11.0 slice_add_fusion
  336.6 12.1 copy.56
  348.7 10.3 reshape.505
  358.9 9.9 copy.57
  368.8 4.7 select_add_fusion
  373.6 3.4 copy-done
  378.1 4.6 slice.186
  382.7 5.2 copy.59
  387.9 5.9 copy.60
  393.8 43.7 %all-reduce.8.cloned.1.call-done = f32[512,512]{0,1:T(8,128)} async-done(((f32[512,512]{0,1:T(8,128)}), f32[512,512]{0,1:T(8,128)}) %all-reduce.8.cloned.1.call-update) | async-done | bytes 1048592 | tf_op jit(solution)/shard_map/psum | solution.py:11
  440.6 11.7 cholesky.286
  452.5 9.8 custom-call.27
  463.0 11.7 cholesky.305
  474.7 10.0 custom-call.28
  485.4 11.7 cholesky.326
  497.8 9.8 custom-call.29
  508.2 11.7 cholesky.343
  524.5 7.8 while.8
  532.3 39.3 %custom-call.30 = f32[4,128,128]{1,2,0:T(8,128)S(1)} custom-call(f32[4,128,128]{2,1,0:T(8,128)S(1)} %get-tuple-element.62), custom_call_target="InvertDiagBlocksLowerTriangular" | custom-call | tf_op jit(solution)/shard_map/jit(_solve_triangular)/triangular_solve | solution.py:67
  571.7 2.4 fusion.42
  574.1 2.2 convolution_subtract_fusion.3
  579.7 2.0 fusion.28
  582.8 2.5 maximum_bitcast_fusion
  585.3 5.3 copy.75
  590.6 4.9 select_select_fusion.1
  595.7 105.2 %all-reduce.10.cloned.1.call-done = f32[4,512,512]{2,1,0:T(8,128)} async-done(((f32[4,512,512]{2,1,0:T(8,128)}), f32[4,512,512]{2,1,0:T(8,128)}) %all-reduce.10.cloned.1.call-update) | async-done | bytes 4194320 | tf_op jit(solution)/shard_map/psum | solution.py:11
  700.8 2.9 gather_fusion.3
  703.7 1.7 select_select_fusion.3
  705.6 5.2 copy.62
  710.8 57.7 %all-reduce.12.cloned.1.call-done = f32[2,512,512]{2,1,0:T(8,128)} async-done(((f32[2,512,512]{2,1,0:T(8,128)}), f32[2,512,512]{2,1,0:T(8,128)}) %all-reduce.12.cloned.1.call-update) | async-done | bytes 2097168 | tf_op jit(solution)/shard_map/psum | solution.py:11
  768.6 17.6 %fusion.2 = f32[4,512,2,512]{1,3,2,0:T(8,128)S(1)} fusion(f32[4,512,2,512]{1,3,2,0:T(8,128)} %copy-done, f32[4,512,512]{1,2,0:T(8,128)} %copy.62, pred[2]{0:T(512)(128)(4,1)S(1)} %get-tuple-element.118, pred[4,2]{1,0:T(4,128)(4,1)S(1)} %get-tuple-element.111, pred[4,2]{1,0:T(4,128)(4,1)S(1)} %get-tuple-element.110, ...), kind=kOutput, calls=%fused_computation.14 | convolution fusion | flops 12893290496 | bytes 27262994 | tf_op jit(solution)/shard_map/dot_general | solution.py:84
  786.2 3.4 copy-done.1
  790.8 4.6 slice.188
  795.3 5.2 copy.65
  800.6 5.6 copy.66
  806.1 46.9 %all-reduce.14.cloned.1.call-done = f32[512,512]{0,1:T(8,128)} async-done(((f32[512,512]{0,1:T(8,128)}), f32[512,512]{0,1:T(8,128)}) %all-reduce.14.cloned.1.call-update) | async-done | bytes 1048592 | tf_op jit(solution)/shard_map/psum | solution.py:11
  856.0 11.7 cholesky.358
  867.9 9.8 custom-call.31
  878.4 11.7 cholesky.377
  891.5 10.0 custom-call.32
  902.1 11.7 cholesky.398
  914.6 9.8 custom-call.33
  925.0 11.7 cholesky.415
  940.6 7.8 while.9
  948.4 39.3 %custom-call.34 = f32[4,128,128]{1,2,0:T(8,128)S(1)} custom-call(f32[4,128,128]{2,1,0:T(8,128)S(1)} %get-tuple-element.63), custom_call_target="InvertDiagBlocksLowerTriangular" | custom-call | tf_op jit(solution)/shard_map/jit(_solve_triangular)/triangular_solve | solution.py:67
  987.7 2.4 fusion.39
  990.2 2.2 convolution_subtract_fusion.2
  995.8 2.0 fusion.25
  998.9 2.5 maximum_bitcast_fusion.1
  1001.4 5.3 copy.67
  1006.7 4.9 select_select_fusion
  1011.8 105.0 %all-reduce.16.cloned.1.call-done = f32[4,512,512]{2,1,0:T(8,128)} async-done(((f32[4,512,512]{2,1,0:T(8,128)}), f32[4,512,512]{2,1,0:T(8,128)}) %all-reduce.16.cloned.1.call-update) | async-done | bytes 4194320 | tf_op jit(solution)/shard_map/psum | solution.py:11
  1116.9 2.9 gather_fusion.4
  1121.6 5.2 copy.68
  1126.8 57.8 %all-reduce.18.cloned.1.call-done = f32[2,512,512]{2,1,0:T(8,128)} async-done(((f32[2,512,512]{2,1,0:T(8,128)}), f32[2,512,512]{2,1,0:T(8,128)}) %all-reduce.18.cloned.1.call-update) | async-done | bytes 2097168 | tf_op jit(solution)/shard_map/psum | solution.py:11
  1184.6 18.7 %fusion.4 = f32[4,512,2,512]{1,3,2,0:T(8,128)} fusion(f32[4,512,2,512]{1,3,2,0:T(8,128)} %copy-done.1, f32[4,512,512]{1,2,0:T(8,128)} %copy.68, pred[2]{0:T(512)(128)(4,1)S(1)} %get-tuple-element.124, pred[4,2]{1,0:T(4,128)(4,1)S(1)} %get-tuple-element.109, pred[4,2]{1,0:T(4,128)(4,1)S(1)} %get-tuple-element.108, ...), kind=kOutput, calls=%fused_computation.16 | convolution fusion | flops 12893290496 | bytes 27262994 | tf_op jit(solution)/shard_map/dot_general | solution.py:84
  1203.3 13.2 %copy.70 = f32[4,512,2,512]{3,2,1,0:T(2,128)} copy(f32[4,512,2,512]{1,3,2,0:T(8,128)} %fusion.4) | data formatting | bytes 16777216 | tf_op jit(solution)/shard_map/jit(_where)/select_n | solution.py:104
  1216.4 8.9 copy.78
  (135 shorter events, 48.1 us)
Async XLA Ops:
  67.9 11.2 copy-start.4
  67.9 257.7 %all-to-all-start = ((f32[128,1,32768]{2,1,0:T(1,128)}), f32[128,1,32768]{2,1,0:T(1,128)}, u32[]{:S(2)}, u32[]{:S(2)}) async-start(f32[128,1,32768]{2,1,0:T(1,128)} %bitcast.154), calls=%async_computation | async-start | bytes 33554432 | tf_op jit(solution)/shard_map/all_to_all | solution.py:46
  78.7 358.8 %all-reduce.8.cloned.1.call-start = ((), (), s32[]{:S(2)}) async-start(), calls=%async_computation.1 | async-start | bytes 2097152 | tf_op jit(solution)/shard_map/psum | solution.py:11
  373.6 3.4 copy-start
  378.1 322.8 %all-reduce.10.cloned.1.call-start = ((), (), s32[]{:S(2)}) async-start(), calls=%async_computation.2 | async-start | bytes 8388608 | tf_op jit(solution)/shard_map/psum | solution.py:11
  571.7 5.7 copy-start.2
  595.5 173.0 %all-reduce.12.cloned.1.call-start = ((), (), s32[]{:S(2)}) async-start(), calls=%async_computation.3 | async-start | bytes 4194304 | tf_op jit(solution)/shard_map/psum | solution.py:11
  705.5 147.6 %all-reduce.14.cloned.1.call-start = ((), (), s32[]{:S(2)}) async-start(), calls=%async_computation.4 | async-start | bytes 2097152 | tf_op jit(solution)/shard_map/psum | solution.py:11
  786.2 3.4 copy-start.1
  790.7 326.2 %all-reduce.16.cloned.1.call-start = ((), (), s32[]{:S(2)}) async-start(), calls=%async_computation.5 | async-start | bytes 8388608 | tf_op jit(solution)/shard_map/psum | solution.py:11
  987.7 5.7 copy-start.3
  1011.6 173.0 %all-reduce.18.cloned.1.call-start = ((), (), s32[]{:S(2)}) async-start(), calls=%async_computation.6 | async-start | bytes 4194304 | tf_op jit(solution)/shard_map/psum | solution.py:11
Sparse Core Ops, SparseCore 0:
  378.2 59.3 all-reduce.7
  595.7 105.1 all-reduce.9
  705.6 62.9 all-reduce.11
  790.8 62.1 all-reduce.13
  1011.7 105.0 all-reduce.15
  1121.6 62.9 all-reduce.17
where the time goes:
time: 1240 us; the launch traced here: 1230 us
  waiting for transfers between devices  662 us (53%)
  other arithmetic  317 us (26%)
  local copies, waits for them, and re-layouts  160 us (13%)
  matrix products  62.2 us (5%)
  between operations  19.3 us (2%)
    psum x6, waiting for transfers between devices, broadcast(): return lax.psum(jnp.where(mine, x, jnp.zeros_like(x)), axis)  416 us
    all_to_all x1, waiting for transfers between devices, shards(): lax.all_to_all(buffer, ('row', 'col'), split_axis=0, concat_axis=0, tiled...  246 us
    another operation x29, other arithmetic, shards(): lower_factor = jnp.linalg.cholesky(diagonal)  158 us
    another operation x5, other arithmetic, shards(): jax.scipy.linalg.solve_triangular(lower_factor, column_slab.reshape(-1, B...  79.9 us
    dot_general x2, matrix products, shards(): lax.dot_general(factor_factor_column.reshape(-1, B), factor_across.reshap...  36.3 us
    select_n x1, other arithmetic, shards(): picked_both = jnp.where(keep_mask, picked_both, 0.0)  29.2 us
  transfers between devices with their start and end apart: 7, of which 7 were waited for; matrix products, arithmetic and copies ran while one was open for 3% of the time, Pallas kernels for 0%

commit v1 on v0

v1 whole, which is shorter than its diff:
```python
import functools

import jax
import jax.numpy as jnp
from jax import lax
from jax.experimental import pallas as pl
from jax.experimental.pallas import tpu as pltpu
from jax.sharding import PartitionSpec as P

B = 512
NB = 32
NCB = 20
N_ROW = 8
N_COL = 16
W = 2 * B
H = 16
SL = 128
CB = 128
ST = 16
HI = lax.Precision.HIGHEST
F32 = jnp.float32
VMEM = pltpu.VMEM
MIB = 1024 * 1024


def whole():
    return pl.BlockSpec(memory_space=VMEM)


def smem():
    return pl.BlockSpec(memory_space=pltpu.SMEM)


def params(mib):
    return pltpu.CompilerParams(vmem_limit_bytes=mib * MIB)


def cost(flops, nbytes):
    return pl.CostEstimate(flops=int(flops), bytes_accessed=int(nbytes), transcendentals=0)


def invert_maps(maps_ref, inv_ref):
    def clear(i, _):
        inv_ref[0, i] = -1
        inv_ref[1, i] = -1
        return 0

    lax.fori_loop(0, NB, clear, 0)

    def fill(b, _):
        inv_ref[0, maps_ref[0, b]] = b
        inv_ref[1, maps_ref[1, b]] = b
        return 0

    lax.fori_loop(0, NCB, fill, 0)


def split_kernel(child_ref, keep_ref, send_ref):
    half = lax.axis_index("row") // (N_ROW // 2)
    turned = jnp.swapaxes(child_ref[0], 0, 1)
    first = turned[:, :H]
    second = turned[:, H:]
    keep_ref[0] = jnp.where(half == 0, first, second)
    send_ref[0] = jnp.where(half == 0, second, first)


def split_child(child):
    shape = jax.ShapeDtypeStruct((NCB, NCB, H, SL), F32)
    spec = pl.BlockSpec((1, NCB, H, SL), lambda a: (a, 0, 0, 0))
    return pl.pallas_call(
        split_kernel,
        grid=(NCB,),
        in_specs=[pl.BlockSpec((1, 2 * H, NCB, SL), lambda a: (a, 0, 0, 0))],
        out_specs=[spec, spec],
        out_shape=[shape, shape],
        compiler_params=params(32),
        cost_estimate=cost(0, 14 * MIB),
        name="split_child",
    )(child)


def panel_kernel(maps_ref, keep_ref, send_ref, xy_ref, d_ref, inv_ref):
    child = lax.axis_index("row") // (N_ROW // 2)
    invert_maps(maps_ref, inv_ref)

    def tile(front_row, front_col, half):
        a = inv_ref[child, front_row]
        b = inv_ref[child, front_col]
        ok = jnp.logical_and(a >= 0, b >= 0)
        a = jnp.maximum(a, 0)
        b = jnp.maximum(b, 0)
        value = jnp.where(half == child, keep_ref[a, b], send_ref[a, b])
        return jnp.where(ok, value, 0.0)

    def across(col, _):
        part, blk, half = col // 4, (col // 2) % 2, col % 2
        for row in range(N_ROW):
            xy_ref[row, col, 0] = tile(row + N_ROW * part, blk, half)
            xy_ref[row, col, 1] = tile(row // 4, col + N_COL * ((row // 2) % 2), row % 2)
        return 0

    lax.fori_loop(0, N_COL, across, 0)
    for blk in range(2):
        for other in range(2):
            for half in range(2):
                d_ref[blk, other, half] = tile(blk, other, half)


def panel_pieces(maps, keep, send):
    return pl.pallas_call(
        panel_kernel,
        in_specs=[smem(), whole(), whole()],
        out_specs=[whole(), whole()],
        out_shape=[
            jax.ShapeDtypeStruct((N_ROW, N_COL, 2, H, SL), F32),
            jax.ShapeDtypeStruct((2, 2, 2, H, SL), F32),
        ],
        scratch_shapes=[pltpu.SMEM((2, NB), jnp.int32)],
        compiler_params=params(32),
        cost_estimate=cost(0, 9 * MIB),
        name="panel_pieces",
    )(maps, keep, send)


def pack_kernel(maps_ref, own_ref, other_ref, out_ref, inv_ref):
    child = lax.axis_index("row") // (N_ROW // 2)
    row = pl.program_id(0)

    @pl.when(row == 0)
    def _():
        invert_maps(maps_ref, inv_ref)

    def value(ref, c, i, j):
        a = inv_ref[c, i]
        b = inv_ref[c, j]
        ok = jnp.logical_and(a >= 0, b >= 0)
        return jnp.where(ok, ref[jnp.maximum(a, 0), jnp.maximum(b, 0)], 0.0)

    def across(col, _):
        for part in range(4):
            for side in range(2):
                i = row + N_ROW * part
                j = col + N_COL * side
                out_ref[0, col, part, side] = value(own_ref, child, i, j) + value(
                    other_ref, 1 - child, i, j
                )
        return 0

    lax.fori_loop(0, N_COL, across, 0)


def pack(maps, own, other):
    return pl.pallas_call(
        pack_kernel,
        grid=(N_ROW,),
        in_specs=[smem(), whole(), whole()],
        out_specs=pl.BlockSpec((1, N_COL, 4, 2, H, SL), lambda r: (r, 0, 0, 0, 0, 0)),
        out_shape=jax.ShapeDtypeStruct((N_ROW, N_COL, 4, 2, H, SL), F32),
        scratch_shapes=[pltpu.SMEM((2, NB), jnp.int32)],
        compiler_params=params(32),
        cost_estimate=cost(0, 16 * MIB),
        name="pack",
    )(maps, own, other)


def dot_tn(a, b):
    return lax.dot_general(a, b, (((0,), (0,)), ((), ())), precision=HI, preferred_element_type=F32)


def dot_nn(a, b):
    return lax.dot_general(a, b, (((1,), (0,)), ((), ())), precision=HI, preferred_element_type=F32)


def dot_nt(a, b):
    return lax.dot_general(a, b, (((1,), (1,)), ((), ())), precision=HI, preferred_element_type=F32)


def factor_block(t_ref, w_ref, s_ref, e_ref):
    for p in range(CB // ST):
        lo = p * ST
        rows = lax.broadcasted_iota(jnp.int32, (ST, CB), 0)
        cols = lax.broadcasted_iota(jnp.int32, (ST, CB), 1)
        ident = jnp.where(cols == rows + lo, 1.0, 0.0).astype(F32)
        s = jnp.concatenate([t_ref[lo : lo + ST, :], ident], axis=1)
        if p:
            s = s - dot_tn(w_ref[0:lo, lo : lo + ST], w_ref[0:lo, :])
        s_ref[...] = s
        for c in range(ST):
            e_ref[c] = jnp.broadcast_to(s[:, lo + c : lo + c + 1], (ST, CB))
        e = {}
        for c in range(ST):
            for r in range(c, ST):
                e[r, c] = e_ref[c, r : r + 1, :]
        done = []
        for j in range(ST):
            inv = lax.rsqrt(e[j, j])
            for r in range(j + 1, ST):
                e[r, j] = e[r, j] * inv
            for c in range(j + 1, ST):
                for r in range(c, ST):
                    e[r, c] = e[r, c] - e[r, j] * e[c, j]
            u = s_ref[j : j + 1, :]
            for m in range(j):
                u = u - jnp.concatenate([e[j, m], e[j, m]], axis=1) * done[m]
            u = u * jnp.concatenate([inv, inv], axis=1)
            done.append(u)
            w_ref[lo + j : lo + j + 1, :] = u


def chol_kernel(d_ref, diag_ref, l_ref, linv_ref, a_s, w_s, s_s, e_s, t_s):
    n = W
    nb = n // CB
    a_s[...] = jnp.zeros_like(a_s)
    for src in range(N_COL):
        for blk in range(2):
            lo = blk * B + src * 2 * H
            a_s[lo : lo + 2 * H, :] = d_ref[src, blk]
    low = lax.broadcasted_iota(jnp.int32, (CB, CB), 0)
    high = lax.broadcasted_iota(jnp.int32, (CB, CB), 1)
    l_ref[...] = jnp.zeros_like(l_ref)
    linv_ref[...] = jnp.zeros_like(linv_ref)

    def block(i):
        return pl.ds(pl.multiple_of(i * CB, CB), CB)

    def add_diagonal(k, _):
        ks = block(k)
        a_s[ks, ks] = a_s[ks, ks] + jnp.where(low == high, diag_ref[0:1, ks], 0.0)
        return 0

    lax.fori_loop(0, nb, add_diagonal, 0)

    def step(k, _):
        ks = block(k)
        t_s[...] = a_s[ks, ks]
        factor_block(t_s, w_s, s_s, e_s)
        upper = jnp.where(low <= high, w_s[:, 0:CB], 0.0)
        lower_inverse = jnp.where(low >= high, w_s[:, CB:], 0.0)

        def solve(j, _):
            js = block(j)
            r = dot_nn(lower_inverse, a_s[ks, js])
            a_s[ks, js] = r
            l_ref[js, ks] = r.T
            return 0

        lax.fori_loop(k + 1, nb, solve, 0)
        l_ref[ks, ks] = upper.T

        def update(i, _):
            ins = block(i)
            f = a_s[ks, ins]

            def inner(j, _):
                js = block(j)
                a_s[ins, js] = a_s[ins, js] - dot_tn(f, a_s[ks, js])
                return 0

            lax.fori_loop(i, nb, inner, 0)
            return 0

        lax.fori_loop(k + 1, nb, update, 0)
        linv_ref[ks, ks] = lower_inverse
        return 0

    lax.fori_loop(0, nb, step, 0)
    for i in range(1, nb):
        lo = i * CB
        acc = dot_nn(l_ref[lo : lo + CB, 0:lo], linv_ref[0:lo, 0:lo])
        linv_ref[lo : lo + CB, 0:lo] = -dot_nn(linv_ref[lo : lo + CB, lo : lo + CB], acc)


def cholesky(d, diag):
    return pl.pallas_call(
        chol_kernel,
        in_specs=[whole(), whole()],
        out_specs=[whole(), whole()],
        out_shape=[jax.ShapeDtypeStruct((W, W), F32)] * 2,
        scratch_shapes=[
            VMEM((W, W), F32),
            VMEM((CB, 2 * CB), F32),
            VMEM((ST, 2 * CB), F32),
            VMEM((ST, ST, CB), F32),
            VMEM((CB, CB), F32),
        ],
        compiler_params=params(40),
        cost_estimate=cost(5e10, 12 * MIB),
        name="leading_cholesky",
    )(d, diag)


def across_kernel(y_ref, linv_ref, high_ref, low_ref, a_s):
    for blk in range(2):
        for half in range(2):
            for src in range(N_COL):
                lo = blk * B + src * 2 * H + half * H
                a_s[lo : lo + H, :] = y_ref[blk, 0, half, src]
    step = 256
    for t in range(W // step):
        lo, hi = t * step, (t + 1) * step
        r = dot_nn(linv_ref[lo:hi, 0:hi], a_s[0:hi, :])
        high = r.astype(jnp.bfloat16)
        high_ref[lo:hi, :] = high
        low_ref[lo:hi, :] = (r - high.astype(F32)).astype(jnp.bfloat16)


def solve_across(y, linv):
    out = jax.ShapeDtypeStruct((W, 2 * B), jnp.bfloat16)
    spec = pl.BlockSpec((W, B), lambda q: (0, q))
    return pl.pallas_call(
        across_kernel,
        grid=(2,),
        in_specs=[
            pl.BlockSpec((2, 1, 2, N_COL, H, B), lambda q: (0, q, 0, 0, 0, 0)),
            whole(),
        ],
        out_specs=[spec, spec],
        out_shape=[out, out],
        scratch_shapes=[VMEM((W, B), F32)],
        compiler_params=params(40),
        cost_estimate=cost(8e9, 12 * MIB),
        name="solve_across",
    )(y, linv)


def product_kernel(x_ref, linv_ref, l_ref, high_ref, low_ref, p_ref, a_s, f_s):
    row = lax.axis_index("row")
    col = lax.axis_index("col")
    part = pl.program_id(0)
    front_row = row + N_ROW * part

    @pl.when(front_row >= 2)
    def _():
        for blk in range(2):
            for half in range(2):
                for src in range(N_COL):
                    lo = src * 2 * H + half * H
                    a_s[lo : lo + H, blk * B : (blk + 1) * B] = x_ref[0, blk, half, src]
        step = 256
        for t in range(W // step):
            lo, hi = t * step, (t + 1) * step
            f_s[:, lo:hi] = dot_nt(a_s[:, 0:hi], linv_ref[lo:hi, 0:hi])
        f = f_s[...]
        f_high = f.astype(jnp.bfloat16)
        f_low = (f - f_high.astype(F32)).astype(jnp.bfloat16)

        def mul(x, y):
            return lax.dot_general(x, y, (((1,), (0,)), ((), ())), preferred_element_type=F32)

        for t in range(W // step):
            ts = slice(t * step, (t + 1) * step)
            high = high_ref[:, ts]
            p_ref[:, ts] = mul(f_high, high) + (mul(f_low, high) + mul(f_high, low_ref[:, ts]))

    @pl.when(front_row < 2)
    def _():
        p_ref[...] = jnp.zeros_like(p_ref)
        f_s[...] = l_ref[pl.ds(pl.multiple_of(jnp.minimum(front_row, 1) * B, B), B), :]

    @pl.when(col == 0)
    def _():
        p_ref[:, 0:B] = -f_s[:, 0:B]

    @pl.when(col == 1)
    def _():
        p_ref[:, 0:B] = -f_s[:, B:]


def panel_product(x, linv, lower, high, low):
    return pl.pallas_call(
        product_kernel,
        grid=(4,),
        in_specs=[
            pl.BlockSpec((1, 2, 2, N_COL, H, B), lambda s: (s, 0, 0, 0, 0, 0)),
            whole(),
            whole(),
            whole(),
            whole(),
        ],
        out_specs=pl.BlockSpec((B, 2 * B), lambda s: (s, 0)),
        out_shape=jax.ShapeDtypeStruct((4 * B, 2 * B), F32),
        scratch_shapes=[VMEM((B, W), F32), VMEM((B, W), F32)],
        compiler_params=params(50),
        cost_estimate=cost(2.5e10, 30 * MIB),
        name="panel_product",
    )(x, linv, lower, high, low)


def finish_kernel(recv_ref, p_ref, diag_ref, out_ref):
    row = lax.axis_index("row")
    col = lax.axis_index("col")
    front_row = row + N_ROW * pl.program_id(0)
    front_col = col + N_COL * pl.program_id(1)
    inside = jnp.logical_and(front_row >= 2, front_col >= 2)
    for half in range(2):
        for js in range(4):
            cs = slice(js * SL, (js + 1) * SL)
            for src in range(N_COL):
                lo = src * 2 * H + half * H
                value = recv_ref[half * 4 + js, src, 0, 0]
                out_ref[lo : lo + H, cs] = jnp.where(inside, value, 0.0) - p_ref[lo : lo + H, cs]

    @pl.when(jnp.logical_and(inside, front_row == front_col))
    def _():
        for t in range(B // SL):
            ts = slice(t * SL, (t + 1) * SL)
            eye = lax.broadcasted_iota(jnp.int32, (SL, SL), 0) == lax.broadcasted_iota(
                jnp.int32, (SL, SL), 1
            )
            d = diag_ref[front_row, :, ts]
            out_ref[ts, ts] = out_ref[ts, ts] + jnp.where(eye, d, 0.0)


def finish(received, product, diag):
    spec = pl.BlockSpec((B, B), lambda s, q: (s, q))
    return pl.pallas_call(
        finish_kernel,
        grid=(4, 2),
        in_specs=[
            pl.BlockSpec((N_ROW, N_COL, 1, 1, H, SL), lambda s, q: (0, 0, s, q, 0, 0)),
            spec,
            whole(),
        ],
        out_specs=spec,
        out_shape=jax.ShapeDtypeStruct((4 * B, 2 * B), F32),
        compiler_params=params(32),
        cost_estimate=cost(0, 24 * MIB),
        name="finish",
    )(received, product, diag)


def shards(child_fronts, parent_diagonal, block_maps):
    half_rows = N_ROW // 2
    keep, send = split_child(child_fronts)
    other = lax.ppermute(send, "row", [(i, (i + half_rows) % N_ROW) for i in range(N_ROW)])
    xy, d = panel_pieces(block_maps, keep, send)

    d = lax.all_gather(d, "row", axis=0, tiled=False)
    d = d[:half_rows] + d[half_rows:]
    d = d.transpose(1, 3, 4, 2, 0, 5).reshape(2, 2 * H, W)
    d = lax.all_gather(d, "col", axis=0, tiled=False)
    lower, inverse = cholesky(d, parent_diagonal[: 2 * B].reshape(1, 2 * B))

    xy = lax.all_to_all(
        xy.reshape(N_ROW * N_COL, 2, H, SL), ("row", "col"), split_axis=0, concat_axis=0, tiled=True
    )
    xy = xy.reshape(2, half_rows, N_COL, 2, H, SL)
    xy = (xy[0] + xy[1]).transpose(2, 1, 3, 0, 4).reshape(2, N_COL, H, B)
    y = lax.all_gather(xy[1], "row", axis=0, tiled=False).reshape(2, 2, 2, N_COL, H, B)
    x = lax.all_gather(xy[0], "col", axis=0, tiled=False).reshape(4, 2, 2, N_COL, H, B)

    packed = pack(block_maps, keep, other)
    received = lax.all_to_all(
        packed.reshape(N_ROW * N_COL, 4, 2, H, SL),
        ("row", "col"),
        split_axis=0,
        concat_axis=0,
        tiled=True,
    ).reshape(N_ROW, N_COL, 4, 2, H, SL)

    high, low = solve_across(y, inverse)
    product = panel_product(x, inverse, lower, high, low)
    return finish(received, product, parent_diagonal.reshape(NB, 1, B))


def solution(mesh):
    return jax.shard_map(
        shards,
        mesh=mesh,
        in_specs=(P(None, "col", None, "row"), P(), P()),
        out_specs=P("row", "col"),
        check_vma=False,
    )
```

time: 1240 us -> 385 us (0.31)
  waiting for transfers between devices: 662 us -> 102 us
  other arithmetic: 317 us -> 0.24 us
  Pallas kernels: 0 us -> 169 us
  local copies, waits for them, and re-layouts: 160 us -> 36.7 us
  matrix products: 62.2 us -> 0 us
  blocking collectives: 0 us -> 54.4 us
    psum x6 -> x0, waiting for transfers between devices: 416 us -> none  [broadcast(): return lax.psum(jnp.where(mine, x, jnp.zeros_like(x)), axis)]
    all_to_all x1, waiting for transfers between devices: 246 us -> 0.01 us  [shards(): lax.all_to_all(packed.reshape(N_ROW * N_COL, 4, 2, H, SL), ('row', 'col')...]
    another operation x34 -> x0, other arithmetic: 238 us -> none  [the longest x29 158 us: shards(): lower_factor = jnp.linalg.cholesky(diagonal)]
    pallas_call x0 -> x7, Pallas kernels: none -> 169 us  [the longest x1 84.7 us: cholesky(): pl.pallas_call(chol_kernel, in_specs=[whole(), whole()], out_specs=[whole...]
    ppermute x0 -> x1, waiting for transfers between devices: none -> 90.4 us  [shards(): lax.ppermute(send, 'row', [(i, (i + half_rows) % N_ROW) for i in range(N_...]
    select_n x12 -> x0, other arithmetic: 54.7 us -> none  [the longest x1 29.2 us: shards(): picked_both = jnp.where(keep_mask, picked_both, 0.0)]
    all_to_all x0 -> x1, blocking collectives: none -> 41.1 us  [shards(): lax.all_to_all(xy.reshape(N_ROW * N_COL, 2, H, SL), ('row', 'col'), split...]
    dot_general x2 -> x0, matrix products: 36.3 us -> none  [shards(): lax.dot_general(factor_factor_column.reshape(-1, B), factor_across.reshap...]
  transfers between devices with their start and end apart: 7 -> 5, of which waited for: 7 -> 2; matrix products, arithmetic and copies ran while one was open for 3% -> 2% of each run, Pallas kernels for 0% -> 40%
where the time goes in v1:
time: 385 us
  Pallas kernels  169 us (44%)
  waiting for transfers between devices  102 us (26%)
  blocking collectives  54.4 us (14%)
  local copies, waits for them, and re-layouts  36.7 us (10%)
  between operations  13.3 us (3%)
  starting transfers between devices  8.98 us (2%)
    ppermute x1, waiting for transfers between devices, shards(): lax.ppermute(send, 'row', [(i, (i + half_rows) % N_ROW) for i in range(N_...  90.4 us
    pallas_call x1, Pallas kernels, cholesky(): pl.pallas_call(chol_kernel, in_specs=[whole(), whole()], out_specs=[whole...  84.7 us
    pallas_call x1, Pallas kernels, panel_product(): pl.pallas_call(product_kernel, grid=(4,), in_specs=[pl.BlockSpec((1, 2, 2...  47.7 us
    all_to_all x1, blocking collectives, shards(): lax.all_to_all(xy.reshape(N_ROW * N_COL, 2, H, SL), ('row', 'col'), split...  41.1 us
    unnamed x25, local copies, waits for them, and re-layouts  29.9 us
    pallas_call x1, Pallas kernels, pack(): pl.pallas_call(pack_kernel, grid=(N_ROW,), in_specs=[smem(), whole(), who...  13.5 us
    all_gather x1, blocking collectives, shards(): d = lax.all_gather(d, 'row', axis=0, tiled=False)  13.3 us
    all_gather x1, waiting for transfers between devices, shards(): lax.all_gather(xy[0], 'col', axis=0, tiled=False)  11.4 us
  transfers between devices with their start and end apart: 5, of which 2 were waited for; matrix products, arithmetic and copies ran while one was open for 2% of the time, Pallas kernels for 40%

profile of v1, /device:TPU:12, one launch (start us, length us, event | category | flops | bytes accessed | tf_op | source)
XLA Modules:
  0.0 384.7 jit_solution(5244809145030542713)
XLA Ops:
  6.5 0.0 all-gather.7.cloned.1.call-start
  6.5 8.1 %copy.7.child_ref = f32[20,32,20,128]{3,2,1,0:T(8,128)S(1)} copy(f32[20,32,20,128]{3,1,2,0:T(8,128)} %param.3) | data formatting | bytes 13107200 | tf_op args[0]
  14.6 0.0 copy-start.5
  14.6 1.5 split_child.1
  16.2 0.0 copy-done.5
  16.2 2.8 panel_pieces.1
  19.0 0.0 copy-start.2
  19.0 1.7 copy-done.2
  20.7 0.0 copy-start.3
  20.7 1.3 copy-done.3
  22.1 13.3 %all-gather = f32[16,2,2,16,128]{4,3,2,1,0:T(8,128)S(1)} all-gather(f32[2,2,2,16,128]{4,3,2,1,0:T(8,128)S(1)} %get-tuple-element.16), channel_id=2, replica_groups=mesh['row'=8,'col'=16] {'row'}, dimensions={0}, use_global_device_ids=true | all-gather | bytes 589824 | tf_op jit(solution)/shard_map/all_gather | solution.py:438
  35.4 0.2 copy.9
  35.6 0.8 all_gather_reshape.3
  36.4 0.0 all-gather.7.cloned.1.call-update
  36.4 0.0 all-gather.9.cloned.1.call-start
  36.5 41.1 %all_to_all.10 = f32[128,2,16,128]{3,2,1,0:T(8,128)S(1)} all-to-all(f32[128,2,16,128]{3,2,1,0:T(8,128)} %bitcast.15), channel_id=1, replica_groups=mesh['row'=8,'col'=16] {'row','col'}, dimensions={0} | all-to-all | bytes 4194304 | tf_op jit(solution)/shard_map/all_to_all | solution.py:444
  77.6 0.2 slice_add_fusion
  77.8 0.7 copy.11
  78.5 1.1 fusion
  79.6 2.1 slice.37
  81.6 0.0 all-gather.9.cloned.1.call-update
  81.7 0.0 all-gather.5.cloned.1.call-start
  81.7 2.1 slice.32
  83.8 0.0 all-gather.5.cloned.1.call-update
  83.8 1.9 collective-permute-start
  85.7 90.4 %collective-permute-done.other_ref = f32[20,20,16,128]{3,2,1,0:T(8,128)S(1)} collective-permute-done((f32[20,20,16,128]{3,2,1,0:T(8,128)}, f32[20,20,16,128]{3,2,1,0:T(8,128)S(1)}, u32[]{:S(2)}, u32[]{:S(2)}) %collective-permute-start) | collective-permute-done | bytes 3276832 | tf_op jit(solution)/shard_map/ppermute | solution.py:435
  176.1 13.5 %pack.1 = f32[8,16,4,2,16,128]{5,4,3,2,1,0:T(8,128)S(1)} custom-call(s32[2,20]{1,0:T(2,128)S(1)} %copy-done.5, f32[20,20,16,128]{3,2,1,0:T(8,128)S(1)} %get-tuple-element.13.own_ref.keep_ref, f32[20,20,16,128]{3,2,1,0:T(8,128)S(1)} %collective-permute-done.other_ref), custom_call_target="tpu_custom_call" | custom-call | bytes 16777216 | tf_op jit(solution)/shard_map/pack/pallas_call | solution.py:153
  189.6 0.0 copy-start
  189.6 3.5 copy-done
  193.1 0.0 copy-start.4
  193.1 7.0 %all-to-all-start = ((f32[128,4,2,16,128]{4,3,2,1,0:T(8,128)}), f32[128,4,2,16,128]{4,3,2,1,0:T(8,128)}, u32[]{:S(2)}, u32[]{:S(2)}) async-start(f32[128,4,2,16,128]{4,3,2,1,0:T(8,128)} %bitcast.14), calls=%async_computation | async-start | bytes 16777216 | tf_op jit(solution)/shard_map/all_to_all | solution.py:453
  200.1 0.0 copy-done.4
  200.1 0.0 all-gather.7.cloned.1.call-done.d_ref
  200.2 0.0 copy-start.6
  200.2 2.2 copy-done.6
  202.4 84.7 %leading_cholesky.1 = (f32[1024,1024]{1,0:T(8,128)S(1)}, f32[1024,1024]{1,0:T(8,128)S(1)}) custom-call(f32[16,2,32,1024]{3,2,1,0:T(8,128)S(1)} %copy-done.6, f32[1,1024]{1,0:T(1,128)S(1)} %bitcast.17), custom_call_target="tpu_custom_call" | custom-call | flops 49999998976 | bytes 12582912 | tf_op jit(solution)/shard_map/leading_cholesky/pallas_call | solution.py:274
  287.1 0.0 copy-start.8
  287.1 2.0 copy-done.8
  289.1 0.0 copy-start.11
  289.1 2.0 copy-done.11
  291.1 0.0 all-gather.9.cloned.1.call-done
  291.1 0.0 copy-start.7
  291.1 2.2 copy-done.7
  293.3 0.0 copy-start.9
  293.3 2.2 copy-done.9
  295.5 9.6 %solve_across.1 = (bf16[1024,1024]{1,0:T(8,128)(2,1)S(1)}, bf16[1024,1024]{1,0:T(8,128)(2,1)S(1)}) custom-call(f32[2,2,2,16,16,512]{5,4,3,2,1,0:T(8,128)S(1)} %bitcast.18, f32[1024,1024]{1,0:T(8,128)S(1)} %copy-done.9), custom_call_target="tpu_custom_call" | custom-call | flops 8000000000 | bytes 12582912 | tf_op jit(solution)/shard_map/solve_across/pallas_call | solution.py:310
  305.1 0.0 copy-start.10
  305.1 1.3 copy-done.10
  306.3 11.4 %all-gather.5.cloned.1.call-done = f32[16,16,16,512]{3,2,1,0:T(8,128)} async-done(((f32[1,16,16,512]{3,2,1,0:T(8,128)}), f32[16,16,16,512]{3,2,1,0:T(8,128)}) %all-gather.5.cloned.1.call-update) | async-done | bytes 8388624 | tf_op jit(solution)/shard_map/all_gather | solution.py:450
  317.7 47.7 %panel_product.1.p_ref = f32[2048,1024]{1,0:T(8,128)} custom-call(f32[4,2,2,16,16,512]{5,4,3,2,1,0:T(8,128)} %bitcast.22, f32[1024,1024]{1,0:T(8,128)} %copy-done.8, f32[1024,1024]{1,0:T(8,128)} %copy-done.11, bf16[1024,1024]{1,0:T(8,128)(2,1)S(1)} %get-tuple-element.19.high_ref, bf16[1024,1024]{1,0:T(8,128)(2,1)} %copy-done.10), custom_call_target="tpu_custom_call" | custom-call | flops 24999999488 | bytes 31457280 | tf_op jit(solution)/shard_map/panel_product/pallas_call | solution.py:370
  365.5 0.0 all-to-all-done
  365.5 0.0 copy-start.1
  365.5 3.4 copy-done.1
  368.8 9.3 %finish.1 = f32[2048,1024]{1,0:T(8,128)} custom-call(f32[8,16,4,2,16,128]{5,4,3,2,1,0:T(8,128)} %bitcast.1.recv_ref, f32[2048,1024]{1,0:T(8,128)S(1)} %copy-done.1, f32[32,1,512]{2,1,0:T(1,128)S(1)} %bitcast.16), custom_call_target="tpu_custom_call" | custom-call | bytes 25165824 | tf_op jit(solution)/shard_map/finish/pallas_call | solution.py:416
  (2 shorter events, 0.0 us)
Async XLA Ops:
  6.5 193.6 %all-gather.7.cloned.1.call-start = ((), (), s32[]{:S(2)}) async-start(), calls=%async_computation.3 | async-start | bytes 4456448 | tf_op jit(solution)/shard_map/all_gather | solution.py:441
  14.6 1.6 copy-start.5
  19.0 1.7 copy-start.2
  20.7 1.3 copy-start.3
  36.4 254.6 %all-gather.9.cloned.1.call-start = ((), (), s32[]{:S(2)}) async-start(), calls=%async_computation.4 | async-start | bytes 4718592 | tf_op jit(solution)/shard_map/all_gather | solution.py:449
  81.7 236.1 %all-gather.5.cloned.1.call-start = ((), (), s32[]{:S(2)}) async-start(), calls=%async_computation.2 | async-start | bytes 8912896 | tf_op jit(solution)/shard_map/all_gather | solution.py:450
  83.8 92.3 %collective-permute-start = (f32[20,20,16,128]{3,2,1,0:T(8,128)}, f32[20,20,16,128]{3,2,1,0:T(8,128)S(1)}, u32[]{:S(2)}, u32[]{:S(2)}) collective-permute-start(f32[20,20,16,128]{3,2,1,0:T(8,128)} %copy-done.2), channel_id=1, source_target_pairs={{0,64},{16,80},{32,96},{48,112},{64,0},{80,16},{96,32},{112,48},{1... | collective-permute-start | bytes 9830408 | tf_op jit(solution)/shard_map/ppermute | solution.py:435
  189.6 3.5 copy-start
  193.1 7.0 %copy-start.4 = (f32[16384]{0:T(1024)S(1)}, f32[16384]{0:T(1024)}, u32[]{:S(2)}) copy-start(f32[16384]{0:T(1024)} %param.4) | copy-start | bytes 196612
  193.1 172.3 %all-to-all-start = ((f32[128,4,2,16,128]{4,3,2,1,0:T(8,128)}), f32[128,4,2,16,128]{4,3,2,1,0:T(8,128)}, u32[]{:S(2)}, u32[]{:S(2)}) async-start(f32[128,4,2,16,128]{4,3,2,1,0:T(8,128)} %bitcast.14), calls=%async_computation | async-start | bytes 16777216 | tf_op jit(solution)/shard_map/all_to_all | solution.py:453
  200.2 2.2 copy-start.6
  287.1 2.0 copy-start.8
  289.1 2.0 copy-start.11
  291.1 2.2 copy-start.7
  293.3 2.2 copy-start.9
  305.1 1.3 copy-start.10
  365.5 3.4 copy-start.1
Sparse Core Ops, SparseCore 0:
  36.6 69.3 all-gather.6
  107.7 48.2 all-gather.8
  158.2 159.5 all-gather.4

commit v2 on v1

v2 whole, which is shorter than its diff:
```python
import functools

import jax
import jax.numpy as jnp
from jax import lax
from jax.experimental import pallas as pl
from jax.experimental.pallas import tpu as pltpu
from jax.sharding import PartitionSpec as P

B = 512
NB = 32
NCB = 20
N_ROW = 8
N_COL = 16
W = 2 * B
H = 16
SL = 128
CB = 128
ST = 16
HI = lax.Precision.HIGHEST
F32 = jnp.float32
VMEM = pltpu.VMEM
MIB = 1024 * 1024


def whole():
    return pl.BlockSpec(memory_space=VMEM)


def smem():
    return pl.BlockSpec(memory_space=pltpu.SMEM)


def params(mib):
    return pltpu.CompilerParams(vmem_limit_bytes=mib * MIB)


def cost(flops, nbytes):
    return pl.CostEstimate(flops=int(flops), bytes_accessed=int(nbytes), transcendentals=0)


def invert_maps(maps_ref, inv_ref):
    def clear(i, _):
        inv_ref[0, i] = NCB
        inv_ref[1, i] = NCB
        return 0

    lax.fori_loop(0, NB, clear, 0)

    def fill(b, _):
        inv_ref[0, maps_ref[0, b]] = b
        inv_ref[1, maps_ref[1, b]] = b
        return 0

    lax.fori_loop(0, NCB, fill, 0)


TRI = (NCB - 1) * (NCB - 2) // 2


def split_panel_kernel(child_ref, keep_ref, send_ref):
    half = lax.axis_index("row") // (N_ROW // 2)
    keep = pl.ds(pl.multiple_of(half * H, H), H)
    send = pl.ds(pl.multiple_of((1 - half) * H, H), H)
    for b in range(2):
        keep_ref[b] = child_ref[:, b, keep]
        send_ref[b] = child_ref[:, b, send]


def split_panel(child):
    shape = jax.ShapeDtypeStruct((2, NCB, H, SL), F32)
    return pl.pallas_call(
        split_panel_kernel,
        grid=(1,),
        in_specs=[pl.BlockSpec((NCB, 2, 2 * H, SL), lambda g: (0, 0, 0, 0))],
        out_specs=[whole(), whole()],
        out_shape=[shape, shape],
        compiler_params=params(58),
        cost_estimate=cost(0, 2 * MIB),
        name="split_panel",
    )(child)


def split_rest_kernel(child_ref, keep_ref, send_ref):
    half = lax.axis_index("row") // (N_ROW // 2)
    keep = pl.ds(pl.multiple_of(half * H, H), H)
    send = pl.ds(pl.multiple_of((1 - half) * H, H), H)
    for a in range(2, NCB):
        at = (a - 1) * (a - 2) // 2
        keep_ref[at : at + a - 1] = child_ref[a, 2 : a + 1, keep]
        send_ref[at : at + a - 1] = child_ref[a, 2 : a + 1, send]


def split_rest(child):
    shape = jax.ShapeDtypeStruct((TRI, H, SL), F32)
    return pl.pallas_call(
        split_rest_kernel,
        in_specs=[whole()],
        out_specs=[whole(), whole()],
        out_shape=[shape, shape],
        compiler_params=params(58),
        cost_estimate=cost(0, 10 * MIB),
        name="split_rest",
    )(child)


def panel_kernel(maps_ref, keep_ref, other_ref, xd_ref, y_ref, sum_ref, inv_ref):
    child = lax.axis_index("row") // (N_ROW // 2)
    invert_maps(maps_ref, inv_ref)

    def tile(ref, c, i, blk):
        a = inv_ref[c, i]
        b = inv_ref[c, blk]
        ok = jnp.maximum(a, b) < NCB
        return jnp.where(ok, ref[jnp.minimum(b, 1), jnp.minimum(a, NCB - 1)], 0.0)

    def collect(i, _):
        for blk in range(2):
            sum_ref[blk, i] = tile(keep_ref, child, i, blk) + tile(other_ref, 1 - child, i, blk)
        return 0

    lax.fori_loop(0, NB, collect, 0)
    for row in range(N_ROW):
        for part in range(4):
            for blk in range(2):
                xd_ref[row, part * 2 + blk] = sum_ref[blk, row + N_ROW * part]
        for at, (blk, other) in enumerate(((0, 0), (0, 1), (1, 1))):
            xd_ref[row, 8 + at] = sum_ref[other, blk]
    for col in range(N_COL):
        for side in range(2):
            for blk in range(2):
                y_ref[col, side, blk] = sum_ref[blk, col + N_COL * side]


def panel_pieces(maps, keep, other):
    return pl.pallas_call(
        panel_kernel,
        in_specs=[smem(), whole(), whole()],
        out_specs=[whole(), whole()],
        out_shape=[
            jax.ShapeDtypeStruct((N_ROW, 11, H, SL), F32),
            jax.ShapeDtypeStruct((N_COL, 2, 2, H, SL), F32),
        ],
        scratch_shapes=[VMEM((2, NB, H, SL), F32), pltpu.SMEM((2, NB), jnp.int32)],
        compiler_params=params(58),
        cost_estimate=cost(0, 3 * MIB),
        name="panel_pieces",
    )(maps, keep, other)


WIDE = NCB + 1


def pack_kernel(maps_ref, p0_ref, p1_ref, r0_ref, r1_ref, out_ref, t0_ref, t1_ref, inv_ref):
    child = lax.axis_index("row") // (N_ROW // 2)
    row = pl.program_id(0)

    @pl.when(row == 0)
    def _():
        invert_maps(maps_ref, inv_ref)
        for p_ref, r_ref, t_ref in ((p0_ref, r0_ref, t0_ref), (p1_ref, r1_ref, t1_ref)):
            for a in range(NCB):
                for b in range(min(a + 1, 2)):
                    t_ref[a * WIDE + b] = p_ref[b, a]
                if a >= 2:
                    at = (a - 1) * (a - 2) // 2
                    t_ref[a * WIDE + 2 : a * WIDE + a + 1] = r_ref[at : at + a - 1]
            t_ref[NCB * WIDE : WIDE * WIDE] = jnp.zeros((WIDE, H, SL), F32)

    rows = [
        (inv_ref[child, row + N_ROW * part], inv_ref[1 - child, row + N_ROW * part])
        for part in range(4)
    ]

    def across(col, _):
        for side in range(2):
            j0 = inv_ref[child, col + N_COL * side]
            j1 = inv_ref[1 - child, col + N_COL * side]
            for part in range(4):
                i0, i1 = rows[part]
                out_ref[0, col, part, side] = (
                    t0_ref[jnp.maximum(i0, j0) * WIDE + jnp.minimum(i0, j0)]
                    + t1_ref[jnp.maximum(i1, j1) * WIDE + jnp.minimum(i1, j1)]
                )
        return 0

    lax.fori_loop(0, N_COL, across, 0, unroll=2)


def pack(maps, p0, p1, r0, r1):
    return pl.pallas_call(
        pack_kernel,
        grid=(N_ROW,),
        in_specs=[smem(), whole(), whole(), whole(), whole()],
        out_specs=pl.BlockSpec((1, N_COL, 4, 2, H, SL), lambda r: (r, 0, 0, 0, 0, 0)),
        out_shape=jax.ShapeDtypeStruct((N_ROW, N_COL, 4, 2, H, SL), F32),
        scratch_shapes=[
            VMEM((WIDE * WIDE, H, SL), F32),
            VMEM((WIDE * WIDE, H, SL), F32),
            pltpu.SMEM((2, NB), jnp.int32),
        ],
        compiler_params=params(58),
        cost_estimate=cost(0, 16 * MIB),
        name="pack",
    )(maps, p0, p1, r0, r1)


def dot_tn(a, b):
    return lax.dot_general(a, b, (((0,), (0,)), ((), ())), precision=HI, preferred_element_type=F32)


def dot_nn(a, b):
    return lax.dot_general(a, b, (((1,), (0,)), ((), ())), precision=HI, preferred_element_type=F32)


def dot_nt(a, b):
    return lax.dot_general(a, b, (((1,), (1,)), ((), ())), precision=HI, preferred_element_type=F32)


def factor_block(t_ref, w_ref, s_ref, e_ref):
    for p in range(CB // ST):
        lo = p * ST
        rows = lax.broadcasted_iota(jnp.int32, (ST, CB), 0)
        cols = lax.broadcasted_iota(jnp.int32, (ST, CB), 1)
        ident = jnp.where(cols == rows + lo, 1.0, 0.0).astype(F32)
        s = jnp.concatenate([t_ref[lo : lo + ST, :], ident], axis=1)
        if p:
            s = s - dot_tn(w_ref[0:lo, lo : lo + ST], w_ref[0:lo, :])
        s_ref[...] = s
        for c in range(ST):
            e_ref[c] = jnp.broadcast_to(s[:, lo + c : lo + c + 1], (ST, CB))
        e = {}
        for c in range(ST):
            for r in range(c, ST):
                e[r, c] = e_ref[c, r : r + 1, :]
        done = []
        for j in range(ST):
            inv = lax.rsqrt(e[j, j])
            for r in range(j + 1, ST):
                e[r, j] = e[r, j] * inv
            for c in range(j + 1, ST):
                for r in range(c, ST):
                    e[r, c] = e[r, c] - e[r, j] * e[c, j]
            u = s_ref[j : j + 1, :]
            for m in range(j):
                u = u - jnp.concatenate([e[j, m], e[j, m]], axis=1) * done[m]
            u = u * jnp.concatenate([inv, inv], axis=1)
            done.append(u)
            w_ref[lo + j : lo + j + 1, :] = u


def gather_rows(a_s, row, col, piece):
    for src in range(N_COL):
        for dev in range(N_ROW):
            lo = row + src * 2 * H + (dev // 4) * H
            at = col + (dev % 4) * SL
            a_s[lo : lo + H, at : at + SL] = piece(src, dev)


DB = 2 * CB


def chol_kernel(d_ref, diag_ref, l_ref, linv_ref, a_s, w_s, s_s, e_s, t_s):
    nb = W // DB
    for at, (blk, other) in enumerate(((0, 0), (0, 1), (1, 1))):
        gather_rows(a_s, blk * B, other * B, lambda src, dev: d_ref[src, dev, at])
    low = lax.broadcasted_iota(jnp.int32, (CB, CB), 0)
    high = lax.broadcasted_iota(jnp.int32, (CB, CB), 1)
    l_ref[...] = jnp.zeros_like(l_ref)
    linv_ref[...] = jnp.zeros_like(linv_ref)
    for t in range(W // CB):
        ts = slice(t * CB, (t + 1) * CB)
        a_s[ts, ts] = a_s[ts, ts] + jnp.where(low == high, diag_ref[0:1, ts], 0.0)

    def block(i):
        return pl.ds(pl.multiple_of(i * DB, DB), DB)

    def factor():
        factor_block(t_s, w_s, s_s, e_s)
        return jnp.where(low <= high, w_s[:, :CB], 0.0), jnp.where(low >= high, w_s[:, CB:], 0.0)

    def step(k, _):
        ks = block(k)
        k0 = pl.ds(pl.multiple_of(k * DB, CB), CB)
        k1 = pl.ds(pl.multiple_of(k * DB + CB, CB), CB)
        t_s[...] = a_s[k0, k0]
        upper, inverse = factor()
        l_ref[k0, k0] = upper.T
        linv_ref[k0, k0] = inverse
        right = dot_nn(inverse, a_s[k0, k1])
        l_ref[k1, k0] = right.T
        t_s[...] = a_s[k1, k1] - dot_tn(right, right)
        between = dot_tn(right, inverse)
        upper, inverse = factor()
        l_ref[k1, k1] = upper.T
        linv_ref[k1, k1] = inverse
        linv_ref[k1, k0] = -dot_nn(inverse, between)

        def solve(j, _):
            js = block(j)
            r = dot_nn(linv_ref[ks, ks], a_s[ks, js])
            a_s[ks, js] = r
            l_ref[js, ks] = r.T
            return 0

        lax.fori_loop(k + 1, nb, solve, 0)

        def update(i, _):
            ins = block(i)

            def inner(j, _):
                js = block(j)
                a_s[ins, js] = a_s[ins, js] - dot_tn(a_s[ks, ins], a_s[ks, js])
                return 0

            lax.fori_loop(i, nb, inner, 0)
            return 0

        lax.fori_loop(k + 1, nb, update, 0)
        return 0

    lax.fori_loop(0, nb, step, 0)
    for i in range(1, nb):
        lo = i * DB
        acc = dot_nn(l_ref[lo : lo + DB, 0:lo], linv_ref[0:lo, 0:lo])
        linv_ref[lo : lo + DB, 0:lo] = -dot_nn(linv_ref[lo : lo + DB, lo : lo + DB], acc)


def cholesky(d, diag):
    return pl.pallas_call(
        chol_kernel,
        in_specs=[whole(), whole()],
        out_specs=[whole(), whole()],
        out_shape=[jax.ShapeDtypeStruct((W, W), F32)] * 2,
        scratch_shapes=[
            VMEM((W, W), F32),
            VMEM((CB, 2 * CB), F32),
            VMEM((ST, 2 * CB), F32),
            VMEM((ST, ST, CB), F32),
            VMEM((CB, CB), F32),
        ],
        compiler_params=params(58),
        cost_estimate=cost(5e10, 12 * MIB),
        name="leading_cholesky",
    )(d, diag)


def across_kernel(y_ref, linv_ref, high_ref, low_ref, a_s, f_s):
    for blk in range(2):
        gather_rows(a_s, 0, blk * B, lambda src, dev: y_ref[dev, src, 0, blk])
    step = 256
    for t in range(W // step):
        lo, hi = t * step, (t + 1) * step
        f_s[lo:hi, :] = dot_nt(linv_ref[lo:hi, 0:hi], a_s[:, 0:hi])
    for t in range(W // step):
        lo, hi = t * step, (t + 1) * step
        r = dot_tn(linv_ref[lo:, lo:hi], f_s[lo:, :])
        high = r.astype(jnp.bfloat16)
        high_ref[lo:hi, :] = high
        low_ref[lo:hi, :] = (r - high.astype(F32)).astype(jnp.bfloat16)


def solve_across(y, linv):
    out = jax.ShapeDtypeStruct((W, 2 * B), jnp.bfloat16)
    spec = pl.BlockSpec((W, B), lambda q: (0, q))
    return pl.pallas_call(
        across_kernel,
        grid=(2,),
        in_specs=[
            pl.BlockSpec((N_ROW, N_COL, 1, 2, H, SL), lambda q: (0, 0, q, 0, 0, 0)),
            whole(),
        ],
        out_specs=[spec, spec],
        out_shape=[out, out],
        scratch_shapes=[VMEM((B, W), F32), VMEM((W, B), F32)],
        compiler_params=params(58),
        cost_estimate=cost(1.6e10, 12 * MIB),
        name="solve_across",
    )(y, linv)


STEP = 256


def product_kernel(x_ref, linv_ref, l_ref, high_ref, low_ref, p_ref, a_s):
    row = lax.axis_index("row")
    col = lax.axis_index("col")
    part = pl.program_id(0)
    front_row = row + N_ROW * part

    @pl.when(front_row >= 2)
    def _():
        for blk in range(2):
            gather_rows(a_s, 0, blk * B, lambda src, dev: x_ref[src, dev, 0, blk])
        f = a_s[...]
        f_high = f.astype(jnp.bfloat16)
        f_low = (f - f_high.astype(F32)).astype(jnp.bfloat16)

        def mul(x, y):
            return lax.dot_general(x, y, (((1,), (0,)), ((), ())), preferred_element_type=F32)

        def columns(start, stop):
            for lo in range(start, stop, STEP):
                ts = slice(lo, lo + STEP)
                high = high_ref[:, ts]
                p_ref[:, ts] = mul(f_high, high) + (mul(f_low, high) + mul(f_high, low_ref[:, ts]))

        columns(B, 2 * B)

        @pl.when(col >= 2)
        def _():
            columns(0, B)

        for panel in range(2):

            @pl.when(col == panel)
            def _():
                for lo in range(0, B, STEP):
                    at = panel * B + lo
                    p_ref[:, lo : lo + STEP] = -dot_nt(
                        a_s[:, : at + STEP], linv_ref[at : at + STEP, : at + STEP]
                    )

    @pl.when(front_row < 2)
    def _():
        p_ref[...] = jnp.zeros_like(p_ref)
        for panel in range(2):

            @pl.when(col == panel)
            def _():
                rows = pl.ds(pl.multiple_of(jnp.minimum(front_row, 1) * B, B), B)
                p_ref[:, 0:B] = -l_ref[rows, panel * B : (panel + 1) * B]


def panel_product(x, linv, lower, high, low):
    return pl.pallas_call(
        product_kernel,
        grid=(4,),
        in_specs=[
            pl.BlockSpec((N_COL, N_ROW, 1, 2, H, SL), lambda s: (0, 0, s, 0, 0, 0)),
            whole(),
            whole(),
            whole(),
            whole(),
        ],
        out_specs=pl.BlockSpec((B, 2 * B), lambda s: (s, 0)),
        out_shape=jax.ShapeDtypeStruct((4 * B, 2 * B), F32),
        scratch_shapes=[VMEM((B, W), F32)],
        compiler_params=params(58),
        cost_estimate=cost(2.5e10, 30 * MIB),
        name="panel_product",
    )(x, linv, lower, high, low)


def finish_kernel(recv_ref, p_ref, diag_ref, out_ref, tile_s):
    row = lax.axis_index("row")
    col = lax.axis_index("col")
    front_row = row + N_ROW * pl.program_id(0)
    front_col = col + N_COL * pl.program_id(1)
    inside = jnp.logical_and(front_row >= 2, front_col >= 2)

    @pl.when(jnp.logical_and(inside, front_row >= front_col))
    def _():
        for half in range(2):
            for js in range(4):
                cs = slice(js * SL, (js + 1) * SL)
                for src in range(N_COL):
                    lo = src * 2 * H + half * H
                    out_ref[lo : lo + H, cs] = (
                        recv_ref[half * 4 + js, src, 0, 0] - p_ref[lo : lo + H, cs]
                    )

    @pl.when(jnp.logical_and(inside, front_row < front_col))
    def _():
        for js in range(4):
            rs = slice(js * SL, (js + 1) * SL)
            for t in range(4):
                for src in range(4):
                    for half in range(2):
                        lo = src * 2 * H + half * H
                        tile_s[js, t, lo : lo + H, :] = recv_ref[half * 4 + js, t * 4 + src, 0, 0]
                ts = slice(t * SL, (t + 1) * SL)
                out_ref[rs, ts] = tile_s[js, t].T - p_ref[rs, ts]

    @pl.when(jnp.logical_not(inside))
    def _():
        out_ref[...] = -p_ref[...]

    @pl.when(jnp.logical_and(inside, front_row == front_col))
    def _():
        for t in range(B // SL):
            ts = slice(t * SL, (t + 1) * SL)
            eye = lax.broadcasted_iota(jnp.int32, (SL, SL), 0) == lax.broadcasted_iota(
                jnp.int32, (SL, SL), 1
            )
            d = diag_ref[front_row, :, ts]
            out_ref[ts, ts] = out_ref[ts, ts] + jnp.where(eye, d, 0.0)


def finish(received, product, diag):
    spec = pl.BlockSpec((B, B), lambda s, q: (s, q))
    return pl.pallas_call(
        finish_kernel,
        grid=(4, 2),
        in_specs=[
            pl.BlockSpec((N_ROW, N_COL, 1, 1, H, SL), lambda s, q: (0, 0, s, q, 0, 0)),
            spec,
            whole(),
        ],
        out_specs=spec,
        out_shape=jax.ShapeDtypeStruct((4 * B, 2 * B), F32),
        scratch_shapes=[VMEM((4, 4, SL, SL), F32)],
        compiler_params=params(58),
        cost_estimate=cost(0, 24 * MIB),
        name="finish",
    )(received, product, diag)


def swap(x):
    half_rows = N_ROW // 2
    return lax.ppermute(x, "row", [(i, (i + half_rows) % N_ROW) for i in range(N_ROW)])


def exchange(x, axes):
    return lax.all_to_all(x, axes, split_axis=0, concat_axis=0, tiled=True)


def shards(child_fronts, parent_diagonal, block_maps):
    child = child_fronts.transpose(0, 2, 1, 3)
    p_keep, p_send = split_panel(child)
    p_other = swap(p_send)
    r_keep, r_send = split_rest(child)
    r_other = swap(r_send)
    xd, y = panel_pieces(block_maps, p_keep, p_other)

    xd = exchange(xd, "row")
    d = lax.all_gather(xd[:, 8:], "col", axis=0, tiled=False)
    lower, inverse = cholesky(d, parent_diagonal[: 2 * B].reshape(1, 2 * B))
    x = lax.all_gather(xd[:, :8].reshape(N_ROW, 4, 2, H, SL), "col", axis=0, tiled=False)
    packed = pack(block_maps, p_keep, p_other, r_keep, r_other)
    y = lax.all_gather(exchange(y, "col"), "row", axis=0, tiled=False)

    received = exchange(packed.reshape(N_ROW * N_COL, 4, 2, H, SL), ("row", "col"))
    received = received.reshape(N_ROW, N_COL, 4, 2, H, SL)

    high, low = solve_across(y, inverse)
    product = panel_product(x, inverse, lower, high, low)
    return finish(received, product, parent_diagonal.reshape(NB, 1, B))


def solution(mesh):
    return jax.shard_map(
        shards,
        mesh=mesh,
        in_specs=(P(None, "col", None, "row"), P(), P()),
        out_specs=P("row", "col"),
        check_vma=False,
    )
```

time: 385 us -> 311 us (0.81); the launches traced: 385 us -> 305 us
  local copies, waits for them, and re-layouts: 36.7 us -> 4.62 us
  Pallas kernels: 169 us -> 139 us
  blocking collectives: 54.4 us -> 33.3 us
  starting transfers between devices: 8.98 us -> 13.5 us
    ppermute x1 -> x2, waiting for transfers between devices: 90.4 us -> 38.2 us  [swap(): lax.ppermute(x, 'row', [(i, (i + half_rows) % N_ROW) for i in range(N_ROW)])]
    all_gather x3, waiting for transfers between devices: 11.4 us -> 63.1 us  [the longest x1 63 us: shards(): lax.all_gather(xd[:, :8].reshape(N_ROW, 4, 2, H, SL), 'col', axis=0, tile...]
    unnamed x25 -> x4, local copies, waits for them, and re-layouts: 29.9 us -> 1.82 us
    pallas_call x1, Pallas kernels: 84.7 us -> 64.9 us  [cholesky(): pl.pallas_call(chol_kernel, in_specs=[whole(), whole()], out_specs=[whole...]
    all_gather x1 -> x0, blocking collectives: 13.3 us -> none  [shards(): d = lax.all_gather(d, 'row', axis=0, tiled=False)]
    pallas_call x3 -> x4, Pallas kernels: 58.8 us -> 49.1 us  [the longest x1 21.5 us: solve_across(): pl.pallas_call(across_kernel, grid=(2,), in_specs=[pl.BlockSpec((N_ROW, N...]
    all_to_all x1 -> x2, blocking collectives: 41.1 us -> 33.3 us  [exchange(): return lax.all_to_all(x, axes, split_axis=0, concat_axis=0, tiled=True)]
  transfers between devices with their start and end apart: 5 -> 6, of which waited for: 2 -> 3; matrix products, arithmetic and copies ran while one was open for 2% -> 1% of each run, Pallas kernels for 40% -> 40%
where the time goes in v2:
time: 311 us; the launch traced here: 305 us
  Pallas kernels  139 us (45%)
  waiting for transfers between devices  101 us (32%)
  blocking collectives  33.3 us (11%)
  starting transfers between devices  13.5 us (4%)
  between operations  13.1 us (4%)
  local copies, waits for them, and re-layouts  4.62 us (1%)
    pallas_call x1, Pallas kernels, cholesky(): pl.pallas_call(chol_kernel, in_specs=[whole(), whole()], out_specs=[whole...  64.9 us
    all_gather x1, waiting for transfers between devices, shards(): lax.all_gather(xd[:, :8].reshape(N_ROW, 4, 2, H, SL), 'col', axis=0, tile...  63 us
    ppermute x2, waiting for transfers between devices, swap(): lax.ppermute(x, 'row', [(i, (i + half_rows) % N_ROW) for i in range(N_ROW)])  38.2 us
    all_to_all x2, blocking collectives, exchange(): return lax.all_to_all(x, axes, split_axis=0, concat_axis=0, tiled=True)  33.3 us
    pallas_call x1, Pallas kernels, solve_across(): pl.pallas_call(across_kernel, grid=(2,), in_specs=[pl.BlockSpec((N_ROW, N...  21.5 us
    pallas_call x1, Pallas kernels, panel_product(): pl.pallas_call(product_kernel, grid=(4,), in_specs=[pl.BlockSpec((N_COL,...  21.1 us
    pallas_call x1, Pallas kernels, finish(): pl.pallas_call(finish_kernel, grid=(4, 2), in_specs=[pl.BlockSpec((N_ROW,...  11 us
    pallas_call x1, Pallas kernels, pack(): pl.pallas_call(pack_kernel, grid=(N_ROW,), in_specs=[smem(), whole(), who...  10.9 us
  transfers between devices with their start and end apart: 6, of which 3 were waited for; matrix products, arithmetic and copies ran while one was open for 1% of the time, Pallas kernels for 40%

profile of v2, /device:TPU:12, one launch (start us, length us, event | category | flops | bytes accessed | tf_op | source)
XLA Modules:
  0.0 305.4 jit_solution(4146301170946382928)
XLA Ops:
  6.5 0.0 all-gather.8.cloned.1.call-start
  6.5 2.0 split_panel.1
  8.5 2.3 collective-permute-start
  10.8 8.9 %collective-permute-done.p1_ref.other_ref = f32[2,20,16,128]{3,2,1,0:T(8,128)S(1)} collective-permute-done((f32[2,20,16,128]{3,2,1,0:T(8,128)}, f32[2,20,16,128]{3,2,1,0:T(8,128)S(1)}, u32[]{:S(2)}, u32[]{:S(2)}) %collective-permute-start) | collective-permute-done | bytes 327712 | tf_op jit(solution)/shard_map/ppermute | solution.py:521
  19.7 0.0 copy-start.1
  19.7 0.7 copy-done.1
  20.4 3.6 %panel_pieces.1 = (f32[8,11,16,128]{3,2,1,0:T(8,128)}, f32[16,2,2,16,128]{4,3,2,1,0:T(8,128)}) custom-call(s32[2,20]{1,0:T(2,128)} %maps_ref.3, f32[2,20,16,128]{3,2,1,0:T(8,128)} %get-tuple-element.15.p0_ref.keep_ref, f32[2,20,16,128]{3,2,1,0:T(8,128)} %copy-done.1), custom_call_target="tpu_custom_call" | custom-call | bytes 3145728 | tf_op jit(solution)/shard_map/panel_pieces/pallas_call | solution.py:136
  23.9 16.0 %all_to_all.15 = f32[8,11,16,128]{3,2,1,0:T(8,128)S(1)} all-to-all(f32[8,11,16,128]{3,2,1,0:T(8,128)} %get-tuple-element.19), channel_id=1, replica_groups=mesh['row'=8,'col'=16] {'row'}, dimensions={0} | all-to-all | bytes 1441792 | tf_op jit(solution)/shard_map/all_to_all | solution.py:525
  39.9 0.7 slice.13
  40.6 0.0 all-gather.8.cloned.1.call-update
  40.7 0.0 all-gather.10.cloned.1.call-start
  40.7 17.3 %all_to_all.16 = f32[16,2,2,16,128]{4,3,2,1,0:T(8,128)} all-to-all(f32[16,2,2,16,128]{4,3,2,1,0:T(8,128)} %get-tuple-element.22), channel_id=1, replica_groups=mesh['row'=8,'col'=16] {'col'}, dimensions={0} | all-to-all | bytes 1048576 | tf_op jit(solution)/shard_map/all_to_all | solution.py:525
  58.0 0.0 all-gather.10.cloned.1.call-update
  58.1 0.0 all-gather.6.cloned.1.call-start
  58.1 0.8 slice.12
  59.0 0.0 all-gather.6.cloned.1.call-update
  59.0 4.6 %split_rest.1 = (f32[171,16,128]{2,1,0:T(8,128)}, f32[171,16,128]{2,1,0:T(8,128)}) custom-call(f32[20,20,32,128]{3,2,1,0:T(8,128)} %bitcast.10), custom_call_target="tpu_custom_call" | custom-call | bytes 10485760 | tf_op jit(solution)/shard_map/split_rest/pallas_call | solution.py:96
  63.6 1.3 collective-permute-start.1
  64.9 1.3 slice.11
  66.2 29.3 %collective-permute-done.1.r1_ref = f32[171,16,128]{2,1,0:T(8,128)S(1)} collective-permute-done((f32[171,16,128]{2,1,0:T(8,128)}, f32[171,16,128]{2,1,0:T(8,128)S(1)}, u32[]{:S(2)}, u32[]{:S(2)}) %collective-permute-start.1) | collective-permute-done | bytes 1400864 | tf_op jit(solution)/shard_map/ppermute | solution.py:521
  95.5 0.0 copy-start
  95.5 1.1 copy-done
  96.6 10.9 %pack.1 = f32[8,16,4,2,16,128]{5,4,3,2,1,0:T(8,128)} custom-call(s32[2,20]{1,0:T(2,128)} %maps_ref.3, f32[2,20,16,128]{3,2,1,0:T(8,128)} %get-tuple-element.15.p0_ref.keep_ref, f32[2,20,16,128]{3,2,1,0:T(8,128)} %copy-done.1, f32[171,16,128]{2,1,0:T(8,128)} %get-tuple-element.17.r0_ref, f32[171,16,128]{2,1,0:T(8,128)} %copy-done), custom_call_target="tpu_custom_call" | custom-call | bytes 16777216 | tf_op jit(solution)/shard_map/pack/pallas_call | solution.py:191
  107.5 9.8 %all-to-all-start = ((f32[128,4,2,16,128]{4,3,2,1,0:T(8,128)}), f32[128,4,2,16,128]{4,3,2,1,0:T(8,128)}, u32[]{:S(2)}, u32[]{:S(2)}) async-start(f32[128,4,2,16,128]{4,3,2,1,0:T(8,128)} %bitcast.8), calls=%async_computation | async-start | bytes 16777216 | tf_op jit(solution)/shard_map/all_to_all | solution.py:525
  117.3 0.0 all-gather.8.cloned.1.call-done
  117.3 64.9 %leading_cholesky.1 = (f32[1024,1024]{1,0:T(8,128)}, f32[1024,1024]{1,0:T(8,128)}) custom-call(f32[16,8,3,16,128]{4,3,2,1,0:T(8,128)} %bitcast.15, f32[1,1024]{1,0:T(1,128)} %bitcast.13), custom_call_target="tpu_custom_call" | custom-call | flops 49999998976 | bytes 12582912 | tf_op jit(solution)/shard_map/leading_cholesky/pallas_call | solution.py:330
  182.2 0.0 all-gather.10.cloned.1.call-done
  182.2 21.5 %solve_across.1 = (bf16[1024,1024]{1,0:T(8,128)(2,1)}, bf16[1024,1024]{1,0:T(8,128)(2,1)}) custom-call(f32[8,16,2,2,16,128]{5,4,3,2,1,0:T(8,128)} %bitcast.14, f32[1024,1024]{1,0:T(8,128)} %get-tuple-element.20.linv_ref), custom_call_target="tpu_custom_call" | custom-call | flops 16000000000 | bytes 12582912 | tf_op jit(solution)/shard_map/solve_across/pallas_call | solution.py:366
  203.7 63.0 %all-gather.6.cloned.1.call-done.x_ref = f32[16,8,4,2,16,128]{5,4,3,2,1,0:T(8,128)} async-done(((f32[1,8,4,2,16,128]{5,4,3,2,1,0:T(8,128)}), f32[16,8,4,2,16,128]{5,4,3,2,1,0:T(8,128)}) %all-gather.6.cloned.1.call-update) | async-done | bytes 8388624 | tf_op jit(solution)/shard_map/all_gather | solution.py:539
  266.7 21.1 %panel_product.1.p_ref = f32[2048,1024]{1,0:T(8,128)} custom-call(f32[16,8,4,2,16,128]{5,4,3,2,1,0:T(8,128)} %all-gather.6.cloned.1.call-done.x_ref, f32[1024,1024]{1,0:T(8,128)} %get-tuple-element.20.linv_ref, f32[1024,1024]{1,0:T(8,128)} %get-tuple-element.21.l_ref, bf16[1024,1024]{1,0:T(8,128)(2,1)} %get-tuple-element.23.high_ref, ...), custom_call_target="tpu_custom_call" | custom-call | flops 24999999488 | bytes 31457280 | tf_op jit(solution)/shard_map/panel_product/pallas_call | solution.py:436
  287.8 0.0 all-to-all-done
  287.8 11.0 %finish.1 = f32[2048,1024]{1,0:T(8,128)} custom-call(f32[8,16,4,2,16,128]{5,4,3,2,1,0:T(8,128)} %bitcast.2.recv_ref, f32[2048,1024]{1,0:T(8,128)} %panel_product.1.p_ref, f32[32,1,512]{2,1,0:T(1,128)} %bitcast.12), custom_call_target="tpu_custom_call" | custom-call | bytes 25165824 | tf_op jit(solution)/shard_map/finish/pallas_call | solution.py:502
Async XLA Ops:
  6.5 110.8 %all-gather.8.cloned.1.call-start = ((), (), s32[]{:S(2)}) async-start(), calls=%async_computation.4 | async-start | bytes 3342336 | tf_op jit(solution)/shard_map/all_gather | solution.py:537
  8.5 11.2 %collective-permute-start = (f32[2,20,16,128]{3,2,1,0:T(8,128)}, f32[2,20,16,128]{3,2,1,0:T(8,128)S(1)}, u32[]{:S(2)}, u32[]{:S(2)}) collective-permute-start(f32[2,20,16,128]{3,2,1,0:T(8,128)} %get-tuple-element.16), channel_id=1, source_target_pairs={{0,64},{16,80},{32,96},{48,112},{64,0},{80,16},{96,32},{112,48},{1... | collective-permute-start | bytes 983048 | tf_op jit(solution)/shard_map/ppermute | solution.py:521
  19.7 0.7 copy-start.1
  40.7 141.6 %all-gather.10.cloned.1.call-start = ((), (), s32[]{:S(2)}) async-start(), calls=%async_computation.5 | async-start | bytes 4718592 | tf_op jit(solution)/shard_map/all_gather | solution.py:541
  58.1 208.7 %all-gather.6.cloned.1.call-start = ((), (), s32[]{:S(2)}) async-start(), calls=%async_computation.3 | async-start | bytes 8912896 | tf_op jit(solution)/shard_map/all_gather | solution.py:539
  63.6 31.9 %collective-permute-start.1 = (f32[171,16,128]{2,1,0:T(8,128)}, f32[171,16,128]{2,1,0:T(8,128)S(1)}, u32[]{:S(2)}, u32[]{:S(2)}) collective-permute-start(f32[171,16,128]{2,1,0:T(8,128)} %get-tuple-element.18), channel_id=1, source_target_pairs={{0,64},{16,80},{32,96},{48,112},{64,0},{80,16},{96,32},{112,48},{1... | collective-permute-start | bytes 4202504 | tf_op jit(solution)/shard_map/ppermute | solution.py:521
  95.5 1.1 copy-start
  107.5 180.3 %all-to-all-start = ((f32[128,4,2,16,128]{4,3,2,1,0:T(8,128)}), f32[128,4,2,16,128]{4,3,2,1,0:T(8,128)}, u32[]{:S(2)}, u32[]{:S(2)}) async-start(f32[128,4,2,16,128]{4,3,2,1,0:T(8,128)} %bitcast.8), calls=%async_computation | async-start | bytes 16777216 | tf_op jit(solution)/shard_map/all_to_all | solution.py:525
Sparse Core Ops, SparseCore 0:
  40.8 48.6 all-gather.7
  91.2 56.4 all-gather.9
  149.8 116.8 all-gather.5

commit v3 on v2

--- a/solution.py
+++ b/solution.py
@@ -19,6 +19,7 @@
 ST = 16
 HI = lax.Precision.HIGHEST
 F32 = jnp.float32
+BF16 = jnp.bfloat16
 VMEM = pltpu.VMEM
 MIB = 1024 * 1024
 
@@ -215,6 +216,19 @@
 
 def dot_nt(a, b):
     return lax.dot_general(a, b, (((1,), (1,)), ((), ())), precision=HI, preferred_element_type=F32)
+
+
+def split(x, high_ref, low_ref, rows, cols=slice(None)):
+    high = x.astype(BF16)
+    high_ref[rows, cols] = high
+    low_ref[rows, cols] = (x - high.astype(F32)).astype(BF16)
+
+
+def dot3(a_high, a_low, b_high, b_low, dims):
+    def mul(x, y):
+        return lax.dot_general(x, y, (dims, ((), ())), preferred_element_type=F32)
+
+    return mul(a_high, b_high) + (mul(a_low, b_high) + mul(a_high, b_low))
 
 
 def factor_block(t_ref, w_ref, s_ref, e_ref):
@@ -258,12 +272,27 @@
 
 
 DB = 2 * CB
-
-
-def chol_kernel(d_ref, diag_ref, l_ref, linv_ref, a_s, w_s, s_s, e_s, t_s):
+SIDE = 4
+SHIFTS = (0, 3, 1, 2)
+
+
+def chol_kernel(
+    d0_ref, d1_ref, d2_ref, d3_ref, d4_ref, diag_ref, l_ref, linv_ref, high_ref, low_ref, a_s, w_s, s_s, e_s, t_s
+):
     nb = W // DB
-    for at, (blk, other) in enumerate(((0, 0), (0, 1), (1, 1))):
-        gather_rows(a_s, blk * B, other * B, lambda src, dev: d_ref[src, dev, at])
+    me = lax.axis_index("col")
+    halves = ((0, d0_ref, 0, 4), (3, d1_ref, 0, 4), (1, d2_ref, 0, 4), (2, d3_ref, 0, 2), (2, d4_ref, 2, 4))
+    for zone, d_ref, first_x, stop_x in halves:
+        for at_x in range(first_x, stop_x):
+            shift = SHIFTS[at_x]
+            src = lax.rem(me // SIDE + zone, SIDE) * SIDE + lax.rem(lax.rem(me, SIDE) + shift, SIDE)
+            for half in range(2):
+                first = src * 2 * H + half * H
+                for js in range(4):
+                    for at, (blk, other) in enumerate(((0, 0), (0, 1), (1, 1))):
+                        rows = pl.ds(pl.multiple_of(blk * B + first, H), H)
+                        lo = other * B + js * SL
+                        a_s[rows, lo : lo + SL] = d_ref[at_x - first_x, half * 4 + js, at]
     low = lax.broadcasted_iota(jnp.int32, (CB, CB), 0)
     high = lax.broadcasted_iota(jnp.int32, (CB, CB), 1)
     l_ref[...] = jnp.zeros_like(l_ref)
@@ -324,14 +353,16 @@
         lo = i * DB
         acc = dot_nn(l_ref[lo : lo + DB, 0:lo], linv_ref[0:lo, 0:lo])
         linv_ref[lo : lo + DB, 0:lo] = -dot_nn(linv_ref[lo : lo + DB, lo : lo + DB], acc)
-
-
-def cholesky(d, diag):
+    for lo in range(0, W, DB):
+        split(dot_tn(linv_ref[lo:, lo : lo + DB], linv_ref[lo:, :]), high_ref, low_ref, slice(lo, lo + DB))
+
+
+def cholesky(pieces, diag):
     return pl.pallas_call(
         chol_kernel,
-        in_specs=[whole(), whole()],
-        out_specs=[whole(), whole()],
-        out_shape=[jax.ShapeDtypeStruct((W, W), F32)] * 2,
+        in_specs=[whole()] * 6,
+        out_specs=[whole()] * 4,
+        out_shape=[jax.ShapeDtypeStruct((W, W), t) for t in (F32, F32, BF16, BF16)],
         scratch_shapes=[
             VMEM((W, W), F32),
             VMEM((CB, 2 * CB), F32),
@@ -342,133 +373,101 @@
         compiler_params=params(58),
         cost_estimate=cost(5e10, 12 * MIB),
         name="leading_cholesky",
-    )(d, diag)
-
-
-def across_kernel(y_ref, linv_ref, high_ref, low_ref, a_s, f_s):
-    for blk in range(2):
-        gather_rows(a_s, 0, blk * B, lambda src, dev: y_ref[dev, src, 0, blk])
-    step = 256
-    for t in range(W // step):
-        lo, hi = t * step, (t + 1) * step
-        f_s[lo:hi, :] = dot_nt(linv_ref[lo:hi, 0:hi], a_s[:, 0:hi])
-    for t in range(W // step):
-        lo, hi = t * step, (t + 1) * step
-        r = dot_tn(linv_ref[lo:, lo:hi], f_s[lo:, :])
-        high = r.astype(jnp.bfloat16)
-        high_ref[lo:hi, :] = high
-        low_ref[lo:hi, :] = (r - high.astype(F32)).astype(jnp.bfloat16)
-
-
-def solve_across(y, linv):
-    out = jax.ShapeDtypeStruct((W, 2 * B), jnp.bfloat16)
-    spec = pl.BlockSpec((W, B), lambda q: (0, q))
-    return pl.pallas_call(
-        across_kernel,
-        grid=(2,),
-        in_specs=[
-            pl.BlockSpec((N_ROW, N_COL, 1, 2, H, SL), lambda q: (0, 0, q, 0, 0, 0)),
-            whole(),
-        ],
-        out_specs=[spec, spec],
-        out_shape=[out, out],
-        scratch_shapes=[VMEM((B, W), F32), VMEM((W, B), F32)],
-        compiler_params=params(58),
-        cost_estimate=cost(1.6e10, 12 * MIB),
-        name="solve_across",
-    )(y, linv)
+    )(*pieces, diag)
 
 
 STEP = 256
 
 
-def product_kernel(x_ref, linv_ref, l_ref, high_ref, low_ref, p_ref, a_s):
+def rows_kernel(x_ref, linv_ref, l_ref, kh_ref, kl_ref, high_ref, low_ref, panel_ref, a_s):
     row = lax.axis_index("row")
     col = lax.axis_index("col")
-    part = pl.program_id(0)
-    front_row = row + N_ROW * part
+    front_row = row + N_ROW * pl.program_id(0)
 
     @pl.when(front_row >= 2)
     def _():
         for blk in range(2):
             gather_rows(a_s, 0, blk * B, lambda src, dev: x_ref[src, dev, 0, blk])
-        f = a_s[...]
-        f_high = f.astype(jnp.bfloat16)
-        f_low = (f - f_high.astype(F32)).astype(jnp.bfloat16)
-
-        def mul(x, y):
-            return lax.dot_general(x, y, (((1,), (0,)), ((), ())), preferred_element_type=F32)
-
-        def columns(start, stop):
-            for lo in range(start, stop, STEP):
-                ts = slice(lo, lo + STEP)
-                high = high_ref[:, ts]
-                p_ref[:, ts] = mul(f_high, high) + (mul(f_low, high) + mul(f_high, low_ref[:, ts]))
-
-        columns(B, 2 * B)
-
-        @pl.when(col >= 2)
-        def _():
-            columns(0, B)
-
+        a = a_s[...]
+        a_high = a.astype(BF16)
+        a_low = (a - a_high.astype(F32)).astype(BF16)
+        for lo in range(0, W, STEP):
+            ts = slice(lo, lo + STEP)
+            n = dot3(a_high, a_low, kh_ref[:, ts], kl_ref[:, ts], ((1,), (0,)))
+            split(n, high_ref, low_ref, slice(None), ts)
         for panel in range(2):
 
             @pl.when(col == panel)
             def _():
                 for lo in range(0, B, STEP):
                     at = panel * B + lo
-                    p_ref[:, lo : lo + STEP] = -dot_nt(
+                    panel_ref[:, lo : lo + STEP] = dot_nt(
                         a_s[:, : at + STEP], linv_ref[at : at + STEP, : at + STEP]
                     )
 
     @pl.when(front_row < 2)
     def _():
-        p_ref[...] = jnp.zeros_like(p_ref)
         for panel in range(2):
 
             @pl.when(col == panel)
             def _():
                 rows = pl.ds(pl.multiple_of(jnp.minimum(front_row, 1) * B, B), B)
-                p_ref[:, 0:B] = -l_ref[rows, panel * B : (panel + 1) * B]
-
-
-def panel_product(x, linv, lower, high, low):
-    return pl.pallas_call(
-        product_kernel,
+                panel_ref[...] = l_ref[rows, panel * B : (panel + 1) * B]
+
+
+def solve_rows(x, inverse, lower, high, low):
+    spec = pl.BlockSpec((B, W), lambda s: (s, 0))
+    return pl.pallas_call(
+        rows_kernel,
         grid=(4,),
-        in_specs=[
-            pl.BlockSpec((N_COL, N_ROW, 1, 2, H, SL), lambda s: (0, 0, s, 0, 0, 0)),
-            whole(),
-            whole(),
-            whole(),
-            whole(),
+        in_specs=[pl.BlockSpec((N_COL, N_ROW, 1, 2, H, SL), lambda s: (0, 0, s, 0, 0, 0))]
+        + [whole()] * 4,
+        out_specs=[spec, spec, pl.BlockSpec((B, B), lambda s: (s, 0))],
+        out_shape=[
+            jax.ShapeDtypeStruct((4 * B, W), BF16),
+            jax.ShapeDtypeStruct((4 * B, W), BF16),
+            jax.ShapeDtypeStruct((4 * B, B), F32),
         ],
-        out_specs=pl.BlockSpec((B, 2 * B), lambda s: (s, 0)),
-        out_shape=jax.ShapeDtypeStruct((4 * B, 2 * B), F32),
         scratch_shapes=[VMEM((B, W), F32)],
         compiler_params=params(58),
-        cost_estimate=cost(2.5e10, 30 * MIB),
-        name="panel_product",
-    )(x, linv, lower, high, low)
-
-
-def finish_kernel(recv_ref, p_ref, diag_ref, out_ref, tile_s):
-    row = lax.axis_index("row")
-    col = lax.axis_index("col")
-    front_row = row + N_ROW * pl.program_id(0)
-    front_col = col + N_COL * pl.program_id(1)
+        cost_estimate=cost(1.5e10, 30 * MIB),
+        name="solve_rows",
+    )(x, inverse, lower, high, low)
+
+
+def finish_kernel(
+    recv_ref, nh_ref, nl_ref, y_ref, panel_ref, diag_ref, out_ref, p_s, tile_s, yh_s, yl_s
+):
+    side = pl.program_id(0)
+    part = pl.program_id(1)
+    front_row = lax.axis_index("row") + N_ROW * part
+    front_col = lax.axis_index("col") + N_COL * side
     inside = jnp.logical_and(front_row >= 2, front_col >= 2)
 
+    @pl.when(part == 0)
+    def _():
+        for blk in range(2):
+            for src in range(N_COL):
+                for dev in range(N_ROW):
+                    lo = src * 2 * H + (dev // 4) * H
+                    at = blk * B + (dev % 4) * SL
+                    split(
+                        y_ref[dev, src, 0, blk], yh_s, yl_s, slice(lo, lo + H), slice(at, at + SL)
+                    )
+
+    @pl.when(inside)
+    def _():
+        for lo in range(0, B, STEP):
+            ts = slice(lo, lo + STEP)
+            p_s[:, ts] = dot3(nh_ref[...], nl_ref[...], yh_s[ts, :], yl_s[ts, :], ((1,), (1,)))
+
     @pl.when(jnp.logical_and(inside, front_row >= front_col))
     def _():
-        for half in range(2):
-            for js in range(4):
-                cs = slice(js * SL, (js + 1) * SL)
-                for src in range(N_COL):
-                    lo = src * 2 * H + half * H
-                    out_ref[lo : lo + H, cs] = (
-                        recv_ref[half * 4 + js, src, 0, 0] - p_ref[lo : lo + H, cs]
-                    )
+        for dev in range(N_ROW):
+            cs = slice((dev % 4) * SL, (dev % 4 + 1) * SL)
+            for src in range(N_COL):
+                lo = src * 2 * H + (dev // 4) * H
+                out_ref[lo : lo + H, cs] = recv_ref[dev, src, 0, 0] - p_s[lo : lo + H, cs]
 
     @pl.when(jnp.logical_and(inside, front_row < front_col))
     def _():
@@ -480,11 +479,15 @@
                         lo = src * 2 * H + half * H
                         tile_s[js, t, lo : lo + H, :] = recv_ref[half * 4 + js, t * 4 + src, 0, 0]
                 ts = slice(t * SL, (t + 1) * SL)
-                out_ref[rs, ts] = tile_s[js, t].T - p_ref[rs, ts]
-
-    @pl.when(jnp.logical_not(inside))
-    def _():
-        out_ref[...] = -p_ref[...]
+                out_ref[rs, ts] = tile_s[js, t].T - p_s[rs, ts]
+
+    @pl.when(front_col < 2)
+    def _():
+        out_ref[...] = panel_ref[...]
+
+    @pl.when(jnp.logical_and(front_row < 2, front_col >= 2))
+    def _():
+        out_ref[...] = jnp.zeros_like(out_ref)
 
     @pl.when(jnp.logical_and(inside, front_row == front_col))
     def _():
@@ -497,23 +500,31 @@
             out_ref[ts, ts] = out_ref[ts, ts] + jnp.where(eye, d, 0.0)
 
 
-def finish(received, product, diag):
-    spec = pl.BlockSpec((B, B), lambda s, q: (s, q))
+def finish(received, high, low, y, panel, diag):
+    rows = pl.BlockSpec((B, W), lambda q, s: (s, 0))
     return pl.pallas_call(
         finish_kernel,
-        grid=(4, 2),
+        grid=(2, 4),
         in_specs=[
-            pl.BlockSpec((N_ROW, N_COL, 1, 1, H, SL), lambda s, q: (0, 0, s, q, 0, 0)),
-            spec,
+            pl.BlockSpec((N_ROW, N_COL, 1, 1, H, SL), lambda q, s: (0, 0, s, q, 0, 0)),
+            rows,
+            rows,
+            pl.BlockSpec((N_ROW, N_COL, 1, 2, H, SL), lambda q, s: (0, 0, q, 0, 0, 0)),
+            pl.BlockSpec((B, B), lambda q, s: (s * (1 - q), 0)),
             whole(),
         ],
-        out_specs=spec,
+        out_specs=pl.BlockSpec((B, B), lambda q, s: (s, q)),
         out_shape=jax.ShapeDtypeStruct((4 * B, 2 * B), F32),
-        scratch_shapes=[VMEM((4, 4, SL, SL), F32)],
-        compiler_params=params(58),
-        cost_estimate=cost(0, 24 * MIB),
+        scratch_shapes=[
+            VMEM((B, B), F32),
+            VMEM((4, 4, SL, SL), F32),
+            VMEM((B, W), BF16),
+            VMEM((B, W), BF16),
+        ],
+        compiler_params=params(58),
+        cost_estimate=cost(1.3e10, 30 * MIB),
         name="finish",
-    )(received, product, diag)
+    )(received, high, low, y, panel, diag)
 
 
 def swap(x):
@@ -523,6 +534,15 @@
 
 def exchange(x, axes):
     return lax.all_to_all(x, axes, split_axis=0, concat_axis=0, tiled=True)
+
+
+def from_shift(x, stride, shift):
+    pairs = []
+    for i in range(N_COL):
+        place = (i // stride) % SIDE
+        target = (place - shift) % SIDE
+        pairs.append((i, i + (target - place) * stride))
+    return lax.ppermute(x, "col", pairs)
 
 
 def shards(child_fronts, parent_diagonal, block_maps):
@@ -534,18 +554,22 @@
     xd, y = panel_pieces(block_maps, p_keep, p_other)
 
     xd = exchange(xd, "row")
-    d = lax.all_gather(xd[:, 8:], "col", axis=0, tiled=False)
-    lower, inverse = cholesky(d, parent_diagonal[: 2 * B].reshape(1, 2 * B))
     x = lax.all_gather(xd[:, :8].reshape(N_ROW, 4, 2, H, SL), "col", axis=0, tiled=False)
+    d = xd[:, 8:]
+    d = jnp.stack([d] + [from_shift(d, 1, shift) for shift in SHIFTS[1:]])
+    before, after = from_shift(d, SIDE, 3), from_shift(d, SIDE, 1)
+    d = (d, before, after, from_shift(before[:2], SIDE, 3), from_shift(after[2:], SIDE, 1))
     packed = pack(block_maps, p_keep, p_other, r_keep, r_other)
+    packed, *d = lax.optimization_barrier((packed, *d))
+    lower, inverse, high, low = cholesky(d, parent_diagonal[: 2 * B].reshape(1, 2 * B))
+    y, _ = lax.optimization_barrier((y, r_other))
     y = lax.all_gather(exchange(y, "col"), "row", axis=0, tiled=False)
+    high, low, panel = solve_rows(x, inverse, lower, high, low)
 
     received = exchange(packed.reshape(N_ROW * N_COL, 4, 2, H, SL), ("row", "col"))
     received = received.reshape(N_ROW, N_COL, 4, 2, H, SL)
 
-    high, low = solve_across(y, inverse)
-    product = panel_product(x, inverse, lower, high, low)
-    return finish(received, product, parent_diagonal.reshape(NB, 1, B))
+    return finish(received, high, low, y, panel, parent_diagonal.reshape(NB, 1, B))
 
 
 def solution(mesh):

time: 311 us -> 295 us (0.949)
  starting transfers between devices: 13.5 us -> 34.7 us
  waiting for transfers between devices: 101 us -> 80.3 us
  blocking collectives: 33.3 us -> 16 us
    all_gather x1, waiting for transfers between devices: 63 us -> 21.1 us  [shards(): lax.all_gather(xd[:, :8].reshape(N_ROW, 4, 2, H, SL), 'col', axis=0, tile...]
    ppermute x0 -> x7, waiting for transfers between devices: none -> 23.6 us  [from_shift(): return lax.ppermute(x, 'col', pairs)]
    all_to_all x2 -> x1, blocking collectives: 33.3 us -> 16 us  [exchange(): return lax.all_to_all(x, axes, split_axis=0, concat_axis=0, tiled=True)]
    ppermute x2, waiting for transfers between devices: 38.2 us -> 21 us  [swap(): lax.ppermute(x, 'row', [(i, (i + half_rows) % N_ROW) for i in range(N_ROW)])]
    all_gather x1, waiting for transfers between devices: 0.01 us -> 14.1 us  [shards(): y = lax.all_gather(exchange(y, 'col'), 'row', axis=0, tiled=False)]
    ppermute x0 -> x7, starting transfers between devices: none -> 10.7 us  [from_shift(): return lax.ppermute(x, 'col', pairs)]
    all_to_all x1 -> x2, starting transfers between devices: 9.79 us -> 20 us  [exchange(): return lax.all_to_all(x, axes, split_axis=0, concat_axis=0, tiled=True)]
    pallas_call x4 -> x3, Pallas kernels: 118 us -> 118 us  [the longest x1 73.8 us: cholesky(): pl.pallas_call(chol_kernel, in_specs=[whole()] * 6, out_specs=[whole()] *...]
  transfers between devices with their start and end apart: 6 -> 13, of which waited for: 3 -> 9; matrix products, arithmetic and copies ran while one was open for 1% -> 1% of each run, Pallas kernels for 40% -> 38%
where the time goes in v3:
time: 295 us; the launch traced here: 289 us
  Pallas kernels  139 us (47%)
  waiting for transfers between devices  80.3 us (27%)
  starting transfers between devices  34.7 us (12%)
  blocking collectives  16 us (5%)
  between operations  13.9 us (5%)
  local copies, waits for them, and re-layouts  5.85 us (2%)
    pallas_call x1, Pallas kernels, cholesky(): pl.pallas_call(chol_kernel, in_specs=[whole()] * 6, out_specs=[whole()] *...  73.8 us
    ppermute x7, waiting for transfers between devices, from_shift(): return lax.ppermute(x, 'col', pairs)  23.6 us
    pallas_call x1, Pallas kernels, finish(): pl.pallas_call(finish_kernel, grid=(2, 4), in_specs=[pl.BlockSpec((N_ROW,...  23 us
    all_gather x1, waiting for transfers between devices, shards(): lax.all_gather(xd[:, :8].reshape(N_ROW, 4, 2, H, SL), 'col', axis=0, tile...  21.1 us
    ppermute x2, waiting for transfers between devices, swap(): lax.ppermute(x, 'row', [(i, (i + half_rows) % N_ROW) for i in range(N_ROW)])  21 us
    pallas_call x1, Pallas kernels, solve_rows(): pl.pallas_call(rows_kernel, grid=(4,), in_specs=[pl.BlockSpec((N_COL, N_R...  20.9 us
    all_to_all x2, starting transfers between devices, exchange(): return lax.all_to_all(x, axes, split_axis=0, concat_axis=0, tiled=True)  20 us
    all_to_all x1, blocking collectives, exchange(): return lax.all_to_all(x, axes, split_axis=0, concat_axis=0, tiled=True)  16 us
  transfers between devices with their start and end apart: 13, of which 9 were waited for; matrix products, arithmetic and copies ran while one was open for 1% of the time, Pallas kernels for 38%

profile of v3, /device:TPU:12, one launch (start us, length us, event | category | flops | bytes accessed | tf_op | source)
XLA Modules:
  0.0 289.5 jit_solution(3593399450190533149)
XLA Ops:
  6.5 0.0 all-gather.4.cloned.1.call-start
  6.5 2.0 split_panel.1
  8.5 2.3 collective-permute-start
  10.8 8.9 %collective-permute-done.p1_ref.other_ref = f32[2,20,16,128]{3,2,1,0:T(8,128)S(1)} collective-permute-done((f32[2,20,16,128]{3,2,1,0:T(8,128)}, f32[2,20,16,128]{3,2,1,0:T(8,128)S(1)}, u32[]{:S(2)}, u32[]{:S(2)}) %collective-permute-start) | collective-permute-done | bytes 327712 | tf_op jit(solution)/shard_map/ppermute | solution.py:532
  19.7 0.0 copy-start.2
  19.7 0.7 copy-done.2
  20.4 3.5 %panel_pieces.1 = (f32[8,11,16,128]{3,2,1,0:T(8,128)}, f32[16,2,2,16,128]{4,3,2,1,0:T(8,128)}) custom-call(s32[2,20]{1,0:T(2,128)} %maps_ref.3, f32[2,20,16,128]{3,2,1,0:T(8,128)} %get-tuple-element.25.p0_ref.keep_ref, f32[2,20,16,128]{3,2,1,0:T(8,128)} %copy-done.2), custom_call_target="tpu_custom_call" | custom-call | bytes 3145728 | tf_op jit(solution)/shard_map/panel_pieces/pallas_call | solution.py:137
  24.0 16.0 %all_to_all.15 = f32[8,11,16,128]{3,2,1,0:T(8,128)S(1)} all-to-all(f32[8,11,16,128]{3,2,1,0:T(8,128)} %get-tuple-element.29), channel_id=1, replica_groups=mesh['row'=8,'col'=16] {'row'}, dimensions={0} | all-to-all | bytes 1441792 | tf_op jit(solution)/shard_map/all_to_all | solution.py:536
  40.0 0.9 slice.23
  40.8 0.0 all-gather.4.cloned.1.call-update
  40.8 4.6 %split_rest.1 = (f32[171,16,128]{2,1,0:T(8,128)}, f32[171,16,128]{2,1,0:T(8,128)}) custom-call(f32[20,20,32,128]{3,2,1,0:T(8,128)} %bitcast.14), custom_call_target="tpu_custom_call" | custom-call | bytes 10485760 | tf_op jit(solution)/shard_map/split_rest/pallas_call | solution.py:97
  45.4 1.4 collective-permute-start.1
  46.9 0.6 collective-permute-start.4
  47.5 2.2 collective-permute-start.3
  49.6 0.0 collective-permute-start.2
  49.6 9.0 %collective-permute-done.4 = f32[8,3,16,128]{3,2,1,0:T(8,128)S(1)} collective-permute-done((f32[8,3,16,128]{3,2,1,0:T(8,128)S(1)}, f32[8,3,16,128]{3,2,1,0:T(8,128)S(1)}, u32[]{:S(2)}, u32[]{:S(2)}) %collective-permute-start.4) | collective-permute-done | bytes 196640 | tf_op jit(solution)/shard_map/ppermute | solution.py:545
  58.6 3.8 %collective-permute-done.3 = f32[8,3,16,128]{3,2,1,0:T(8,128)S(1)} collective-permute-done((f32[8,3,16,128]{3,2,1,0:T(8,128)S(1)}, f32[8,3,16,128]{3,2,1,0:T(8,128)S(1)}, u32[]{:S(2)}, u32[]{:S(2)}) %collective-permute-start.3) | collective-permute-done | bytes 196640 | tf_op jit(solution)/shard_map/ppermute | solution.py:545
  62.3 0.2 collective-permute-done.2
  62.6 0.1 pad_maximum_fusion.d0_ref
  62.6 0.0 copy-start.3
  62.6 2.2 collective-permute-start.5
  64.8 2.4 collective-permute-start.6
  67.2 12.1 %collective-permute-done.1.r1_ref = f32[171,16,128]{2,1,0:T(8,128)S(1)} collective-permute-done((f32[171,16,128]{2,1,0:T(8,128)}, f32[171,16,128]{2,1,0:T(8,128)S(1)}, u32[]{:S(2)}, u32[]{:S(2)}) %collective-permute-start.1) | collective-permute-done | bytes 1400864 | tf_op jit(solution)/shard_map/ppermute | solution.py:532
  79.3 0.0 copy-start.1
  79.3 8.3 %all-to-all-start.2 = ((f32[16,2,2,16,128]{4,3,2,1,0:T(8,128)}), f32[16,2,2,16,128]{4,3,2,1,0:T(8,128)S(1)}, u32[]{:S(2)}, u32[]{:S(2)}) async-start(f32[16,2,2,16,128]{4,3,2,1,0:T(8,128)} %get-tuple-element.43), calls=%async_computation.2 | async-start | bytes 1048576 | tf_op jit(solution)/shard_map/all_to_all | solution.py:536
  87.6 3.9 %collective-permute-done.5.d1_ref = f32[4,8,3,16,128]{4,3,2,1,0:T(8,128)} collective-permute-done((f32[4,8,3,16,128]{4,3,2,1,0:T(8,128)S(1)}, f32[4,8,3,16,128]{4,3,2,1,0:T(8,128)}, u32[]{:S(2)}, u32[]{:S(2)}) %collective-permute-start.5) | collective-permute-done | bytes 786464 | tf_op jit(solution)/shard_map/ppermute | solution.py:545
  91.5 1.0 slice.21
  92.5 0.1 collective-permute-start.7
  92.6 0.0 collective-permute-done.6.d2_ref
  92.6 1.0 slice.22
  93.6 3.3 %collective-permute-start.8 = (f32[2,8,3,16,128]{4,3,2,1,0:T(8,128)S(1)}, f32[2,8,3,16,128]{4,3,2,1,0:T(8,128)}, u32[]{:S(2)}, u32[]{:S(2)}) collective-permute-start(f32[2,8,3,16,128]{4,3,2,1,0:T(8,128)S(1)} %slice.22), channel_id=1, source_target_pairs={{0,12},{1,13},{2,14},{3,15},{4,0},{5,1},{6,2},{7,3},{8,4},{9,5},{1... | collective-permute-start | bytes 1179656 | tf_op jit(solution)/shard_map/ppermute | solution.py:545
  96.9 0.0 copy-done.1
  96.9 10.9 %pack.1 = f32[8,16,4,2,16,128]{5,4,3,2,1,0:T(8,128)} custom-call(s32[2,20]{1,0:T(2,128)} %maps_ref.3, f32[2,20,16,128]{3,2,1,0:T(8,128)} %get-tuple-element.25.p0_ref.keep_ref, f32[2,20,16,128]{3,2,1,0:T(8,128)} %copy-done.2, f32[171,16,128]{2,1,0:T(8,128)} %get-tuple-element.27.r0_ref, f32[171,16,128]{2,1,0:T(8,128)} %copy-done.1), custom_call_target="tpu_custom_call" | custom-call | bytes 16777216 | tf_op jit(solution)/shard_map/pack/pallas_call | solution.py:192
  107.8 0.0 copy-done.3
  107.8 6.8 %collective-permute-done.7.d3_ref = f32[2,8,3,16,128]{4,3,2,1,0:T(8,128)S(1)} collective-permute-done((f32[2,8,3,16,128]{4,3,2,1,0:T(8,128)S(1)}, f32[2,8,3,16,128]{4,3,2,1,0:T(8,128)S(1)}, u32[]{:S(2)}, u32[]{:S(2)}) %collective-permute-start.7) | collective-permute-done | bytes 393248 | tf_op jit(solution)/shard_map/ppermute | solution.py:545
  114.6 0.0 copy-start.4
  114.6 0.0 collective-permute-done.8.d4_ref
  114.6 0.0 all-to-all-done.2
  114.6 0.0 copy-start
  114.6 0.7 copy-done.4
  115.3 0.2 copy-done
  115.5 11.7 %all-to-all-start.1 = ((f32[128,4,2,16,128]{4,3,2,1,0:T(8,128)}), f32[128,4,2,16,128]{4,3,2,1,0:T(8,128)}, u32[]{:S(2)}, u32[]{:S(2)}) async-start(f32[128,4,2,16,128]{4,3,2,1,0:T(8,128)} %bitcast.12), calls=%async_computation.1 | async-start | bytes 16777216 | tf_op jit(solution)/shard_map/all_to_all | solution.py:536
  127.2 0.2 all-gather.6.cloned.1.call-start
  127.5 0.5 all-gather.6.cloned.1.call-update
  128.0 1.3 slice.19
  129.3 73.8 %leading_cholesky.1 = (f32[1024,1024]{1,0:T(8,128)}, f32[1024,1024]{1,0:T(8,128)}, bf16[1024,1024]{1,0:T(8,128)(2,1)}, bf16[1024,1024]{1,0:T(8,128)(2,1)}) custom-call(f32[4,8,3,16,128]{4,3,2,1,0:T(8,128)} %copy-done.3, f32[4,8,3,16,128]{4,3,2,1,0:T(8,128)} %collective-permute-done.5.d1_ref, f32[4,8,3,16,128]{4,3,2,1,0:T(8,128)} %collective-permute-done.6.d2_ref, ...), custom_call_target="tpu_custom_call" | custom-call | flops 49999998976 | bytes 12582912 | tf_op jit(solution)/shard_map/leading_cholesky/pallas_call | solution.py:361
  203.1 21.1 %all-gather.4.cloned.1.call-done.x_ref = f32[16,8,4,2,16,128]{5,4,3,2,1,0:T(8,128)} async-done(((f32[1,8,4,2,16,128]{5,4,3,2,1,0:T(8,128)}), f32[16,8,4,2,16,128]{5,4,3,2,1,0:T(8,128)}) %all-gather.4.cloned.1.call-update) | async-done | bytes 8388624 | tf_op jit(solution)/shard_map/all_gather | solution.py:557
  224.2 20.9 %solve_rows.1 = (bf16[2048,1024]{1,0:T(8,128)(2,1)}, bf16[2048,1024]{1,0:T(8,128)(2,1)}, f32[2048,512]{1,0:T(8,128)}) custom-call(f32[16,8,4,2,16,128]{5,4,3,2,1,0:T(8,128)} %all-gather.4.cloned.1.call-done.x_ref, f32[1024,1024]{1,0:T(8,128)} %get-tuple-element.36.linv_ref, f32[1024,1024]{1,0:T(8,128)} %get-tuple-element.37.l_ref, ...), custom_call_target="tpu_custom_call" | custom-call | flops 15000000512 | bytes 31457280 | tf_op jit(solution)/shard_map/solve_rows/pallas_call | solution.py:420
  245.1 14.1 %all-gather.6.cloned.1.call-done = f32[128,2,2,16,128]{4,3,2,1,0:T(8,128)} async-done(((f32[16,2,2,16,128]{4,3,2,1,0:T(8,128)}), f32[128,2,2,16,128]{4,3,2,1,0:T(8,128)}) %all-gather.6.cloned.1.call-update) | async-done | bytes 4194320 | tf_op jit(solution)/shard_map/all_gather | solution.py:566
  259.2 0.0 all-to-all-done.1
  259.2 23.0 %finish.1 = f32[2048,1024]{1,0:T(8,128)} custom-call(f32[8,16,4,2,16,128]{5,4,3,2,1,0:T(8,128)} %bitcast.6.recv_ref, bf16[2048,1024]{1,0:T(8,128)(2,1)} %get-tuple-element.40.nh_ref, bf16[2048,1024]{1,0:T(8,128)(2,1)} %get-tuple-element.41.nl_ref, f32[8,16,2,2,16,128]{5,4,3,2,1,0:T(8,128)} %bitcast.21, f32[2048,512]{1,0:T(8,128)} %get-tuple-element.44.panel_ref, ...), custom_call_target="tpu_custom_call" | custom-call | flops 12999999488 | bytes 31457280 | tf_op jit(solution)/shard_map/finish/pallas_call | solution.py:505
  (1 shorter events, 0.0 us)
Async XLA Ops:
  6.5 217.7 %all-gather.4.cloned.1.call-start = ((), (), s32[]{:S(2)}) async-start(), calls=%async_computation.3 | async-start | bytes 8912896 | tf_op jit(solution)/shard_map/all_gather | solution.py:557
  8.5 11.2 %collective-permute-start = (f32[2,20,16,128]{3,2,1,0:T(8,128)}, f32[2,20,16,128]{3,2,1,0:T(8,128)S(1)}, u32[]{:S(2)}, u32[]{:S(2)}) collective-permute-start(f32[2,20,16,128]{3,2,1,0:T(8,128)} %get-tuple-element.26), channel_id=1, source_target_pairs={{0,64},{16,80},{32,96},{48,112},{64,0},{80,16},{96,32},{112,48},{1... | collective-permute-start | bytes 983048 | tf_op jit(solution)/shard_map/ppermute | solution.py:532
  19.7 0.7 copy-start.2
  45.4 33.9 %collective-permute-start.1 = (f32[171,16,128]{2,1,0:T(8,128)}, f32[171,16,128]{2,1,0:T(8,128)S(1)}, u32[]{:S(2)}, u32[]{:S(2)}) collective-permute-start(f32[171,16,128]{2,1,0:T(8,128)} %get-tuple-element.28), channel_id=1, source_target_pairs={{0,64},{16,80},{32,96},{48,112},{64,0},{80,16},{96,32},{112,48},{1... | collective-permute-start | bytes 4202504 | tf_op jit(solution)/shard_map/ppermute | solution.py:532
  46.9 11.7 %collective-permute-start.4 = (f32[8,3,16,128]{3,2,1,0:T(8,128)S(1)}, f32[8,3,16,128]{3,2,1,0:T(8,128)S(1)}, u32[]{:S(2)}, u32[]{:S(2)}) collective-permute-start(f32[8,3,16,128]{3,2,1,0:T(8,128)S(1)} %get-tuple-element.46), channel_id=1, source_target_pairs={{0,2},{1,3},{2,0},{3,1},{4,6},{5,7},{6,4},{7,5},{8,10},{9,11},{10,... | collective-permute-start | bytes 589832 | tf_op jit(solution)/shard_map/ppermute | solution.py:545
  47.5 14.9 %collective-permute-start.3 = (f32[8,3,16,128]{3,2,1,0:T(8,128)S(1)}, f32[8,3,16,128]{3,2,1,0:T(8,128)S(1)}, u32[]{:S(2)}, u32[]{:S(2)}) collective-permute-start(f32[8,3,16,128]{3,2,1,0:T(8,128)S(1)} %get-tuple-element.46), channel_id=1, source_target_pairs={{0,3},{1,0},{2,1},{3,2},{4,7},{5,4},{6,5},{7,6},{8,11},{9,8},{10,9... | collective-permute-start | bytes 589832 | tf_op jit(solution)/shard_map/ppermute | solution.py:545
  49.6 12.9 %collective-permute-start.2 = (f32[8,3,16,128]{3,2,1,0:T(8,128)S(1)}, f32[8,3,16,128]{3,2,1,0:T(8,128)S(1)}, u32[]{:S(2)}, u32[]{:S(2)}) collective-permute-start(f32[8,3,16,128]{3,2,1,0:T(8,128)S(1)} %get-tuple-element.46), channel_id=1, source_target_pairs={{0,1},{1,2},{2,3},{3,0},{4,5},{5,6},{6,7},{7,4},{8,9},{9,10},{10,1... | collective-permute-start | bytes 589832 | tf_op jit(solution)/shard_map/ppermute | solution.py:545
  62.6 45.2 %copy-start.3 = (f32[4,8,3,16,128]{4,3,2,1,0:T(8,128)}, f32[4,8,3,16,128]{4,3,2,1,0:T(8,128)S(1)}, u32[]{:S(2)}) copy-start(f32[4,8,3,16,128]{4,3,2,1,0:T(8,128)S(1)} %pad_maximum_fusion.d0_ref) | copy-start | bytes 2359300
  62.6 28.9 %collective-permute-start.5 = (f32[4,8,3,16,128]{4,3,2,1,0:T(8,128)S(1)}, f32[4,8,3,16,128]{4,3,2,1,0:T(8,128)}, u32[]{:S(2)}, u32[]{:S(2)}) collective-permute-start(f32[4,8,3,16,128]{4,3,2,1,0:T(8,128)S(1)} %pad_maximum_fusion.d0_ref), channel_id=1, source_target_pairs={{0,4},{1,5},{2,6},{3,7},{4,8},{5,9},{6,10},{7,11},{8,12},{9,13},{1... | collective-permute-start | bytes 2359304 | tf_op jit(solution)/shard_map/ppermute | solution.py:545
  64.8 27.8 %collective-permute-start.6 = (f32[4,8,3,16,128]{4,3,2,1,0:T(8,128)S(1)}, f32[4,8,3,16,128]{4,3,2,1,0:T(8,128)}, u32[]{:S(2)}, u32[]{:S(2)}) collective-permute-start(f32[4,8,3,16,128]{4,3,2,1,0:T(8,128)S(1)} %pad_maximum_fusion.d0_ref), channel_id=1, source_target_pairs={{0,12},{1,13},{2,14},{3,15},{4,0},{5,1},{6,2},{7,3},{8,4},{9,5},{1... | collective-permute-start | bytes 2359304 | tf_op jit(solution)/shard_map/ppermute | solution.py:545
  79.3 17.6 %copy-start.1 = (f32[171,16,128]{2,1,0:T(8,128)}, f32[171,16,128]{2,1,0:T(8,128)S(1)}, u32[]{:S(2)}) copy-start(f32[171,16,128]{2,1,0:T(8,128)S(1)} %collective-permute-done.1.r1_ref) | copy-start | bytes 4202500
  79.3 35.3 %all-to-all-start.2 = ((f32[16,2,2,16,128]{4,3,2,1,0:T(8,128)}), f32[16,2,2,16,128]{4,3,2,1,0:T(8,128)S(1)}, u32[]{:S(2)}, u32[]{:S(2)}) async-start(f32[16,2,2,16,128]{4,3,2,1,0:T(8,128)} %get-tuple-element.43), calls=%async_computation.2 | async-start | bytes 1048576 | tf_op jit(solution)/shard_map/all_to_all | solution.py:536
  92.5 22.1 %collective-permute-start.7 = (f32[2,8,3,16,128]{4,3,2,1,0:T(8,128)S(1)}, f32[2,8,3,16,128]{4,3,2,1,0:T(8,128)S(1)}, u32[]{:S(2)}, u32[]{:S(2)}) collective-permute-start(f32[2,8,3,16,128]{4,3,2,1,0:T(8,128)S(1)} %slice.21), channel_id=1, source_target_pairs={{0,4},{1,5},{2,6},{3,7},{4,8},{5,9},{6,10},{7,11},{8,12},{9,13},{1... | collective-permute-start | bytes 1179656 | tf_op jit(solution)/shard_map/ppermute | solution.py:545
  93.6 21.0 %collective-permute-start.8 = (f32[2,8,3,16,128]{4,3,2,1,0:T(8,128)S(1)}, f32[2,8,3,16,128]{4,3,2,1,0:T(8,128)}, u32[]{:S(2)}, u32[]{:S(2)}) collective-permute-start(f32[2,8,3,16,128]{4,3,2,1,0:T(8,128)S(1)} %slice.22), channel_id=1, source_target_pairs={{0,12},{1,13},{2,14},{3,15},{4,0},{5,1},{6,2},{7,3},{8,4},{9,5},{1... | collective-permute-start | bytes 1179656 | tf_op jit(solution)/shard_map/ppermute | solution.py:545
  114.6 0.8 copy-start.4
  114.6 0.9 copy-start
  115.5 143.7 %all-to-all-start.1 = ((f32[128,4,2,16,128]{4,3,2,1,0:T(8,128)}), f32[128,4,2,16,128]{4,3,2,1,0:T(8,128)}, u32[]{:S(2)}, u32[]{:S(2)}) async-start(f32[128,4,2,16,128]{4,3,2,1,0:T(8,128)} %bitcast.12), calls=%async_computation.1 | async-start | bytes 16777216 | tf_op jit(solution)/shard_map/all_to_all | solution.py:536
  127.2 131.9 %all-gather.6.cloned.1.call-start = ((), (), s32[]{:S(2)}) async-start(), calls=%async_computation.4 | async-start | bytes 4718592 | tf_op jit(solution)/shard_map/all_gather | solution.py:566
Sparse Core Ops, SparseCore 0:
  41.0 183.1 all-gather.3
  225.9 33.2 all-gather.5
